TPU v7x, 32 devices: a whole 2x2x4 slice. The times are simulated.
32 devices in a mesh: ens: 2 (over y), node: 4 (over z), feat: 4 (over x, core).
Axes of the slice: x: 2, y: 2, z: 4, core: 2. Of those that a mesh axis runs over, the one named last changes fastest.
Arguments:
- nodes: bfloat16 [4096, 512], P(('ens', 'node', 'feat')), parts along dimension 0, may hold values from -6 to 6
- edges: bfloat16 [65536, 512], P(('ens', 'node', 'feat')), parts along dimension 0, may hold values from -6 to 6
- near_table: int32 [32, 5, 48], P(('ens', 'node', 'feat')), parts along dimension 0, may hold values from 0 to 127, as said below
- far_table: int32 [32, 16, 2], P(('ens', 'node', 'feat')), parts along dimension 0, may hold values from 0 to 127, as said below
- edge_sender: int32 [65536], P(('ens', 'node', 'feat')), parts along dimension 0, may hold values from 0 to 271, as said below
- edge_receiver: int32 [65536], P(('ens', 'node', 'feat')), parts along dimension 0, may hold values from 0 to 271, as said below
- edge_w1: bfloat16 [2, 1536, 512], replicated, may hold values from -0.15625 to 0.15625
- edge_b1: float32 [2, 512], replicated, may hold values from -4 to 4
- edge_w2: bfloat16 [2, 512, 512], replicated, may hold values from -0.25 to 0.25
- edge_gain: float32 [2, 512], replicated, may hold values from 0.5 to 1.5
- edge_shift: float32 [2, 512], replicated, may hold values from -3 to 3
- node_w1: bfloat16 [2, 1024, 512], replicated, may hold values from -0.1875 to 0.1875
- node_b1: float32 [2, 512], replicated, may hold values from -4 to 4
- node_w2: bfloat16 [2, 512, 512], replicated, may hold values from -0.25 to 0.25
- node_gain: float32 [2, 512], replicated, may hold values from 0.5 to 1.5
- node_shift: float32 [2, 512], replicated, may hold values from -3 to 3
Outputs:
- node_out: bfloat16 [4096, 512], P(('ens', 'node', 'feat')), parts along dimension 0
- edge_out: bfloat16 [65536, 512], P(('ens', 'node', 'feat')), parts along dimension 0
There are 2 independent parts, one for each index of `ens`. A program takes and returns all parts, laid end to end along the dimension named above; an argument that names none is the same for every part. Nothing has to cross between parts.
Inputs may be any that keep to these rules, and one draw needn't show every extreme that they name: `near_table`: entry [p, k, c] is a row among the 128 nodes of device p. `far_table`: entry [p, q, c] is a row among the 128 nodes of device p. `edge_sender`: an edge's entry names a near slot (below (5) * 48) or a far slot of the tables as the steps read them. `edge_receiver`: an edge's entry names a near slot (below (5) * 48) or a far slot of the tables as the steps read them.
All inputs are finite; a program needn't handle non-finite values.
Results may differ from a plain program's by a relative error of at most 0.012.
Values may be sent and summed in bfloat16 or wider, within the bound.
A program may use at most 64 MiB of HBM per device.

v0:
```python
import jax
import jax.numpy as jnp
from jax import lax
from jax.sharding import PartitionSpec as P

EPSILON = 1e-05


def passed_along(block, axis, distance):
    devices = range(lax.axis_size(axis))
    route = [((i - distance) % len(devices), i) for i in devices]
    return lax.ppermute(block, axis, route)


def layer_norm(values, norm_gain, norm_shift):
    center = values - jnp.mean(values, axis=-1, keepdims=True)
    spread = jnp.mean(center * center, axis=-1, keepdims=True)
    return center * lax.rsqrt(spread + EPSILON) * norm_gain + norm_shift


def finish(old_state, mixed_rows, norm_gain, norm_shift):
    return (old_state.astype(jnp.float32) + layer_norm(mixed_rows, norm_gain, norm_shift)).astype(
        jnp.bfloat16
    )


def second_half(pre_act, bias_row, second_weight):
    hidden = jax.nn.silu(pre_act + bias_row).astype(jnp.bfloat16)
    return jnp.dot(hidden, second_weight, preferred_element_type=jnp.float32)


def move_rows(block, offset):
    return passed_along(block, ("node", "feat"), offset)


def return_sums(block, offset):
    return passed_along(block.astype(jnp.bfloat16), ("node", "feat"), offset).astype(block.dtype)


def on_device(
    nodes,
    edges,
    near_table,
    far_table,
    edge_sender,
    edge_receiver,
    edge_w1,
    edge_b1,
    edge_w2,
    edge_gain,
    edge_shift,
    node_w1,
    node_b1,
    node_w2,
    node_gain,
    node_shift,
):
    peer_count = lax.axis_size(("node", "feat"))
    span = near_table.shape[1]
    reach = (span - 1) // 2
    near_width = near_table.shape[2]
    near_total = span * near_width
    near_flat = near_table.reshape(near_total)
    slot_width = far_table.shape[2]
    far_total = peer_count * slot_width
    far_flat = far_table.reshape(far_total)
    slot_total = near_total + far_total
    owner_rows = jnp.concatenate([near_flat, far_flat])
    node_rows = nodes.shape[0]
    features = nodes.shape[1]
    layer_count = edge_w1.shape[0]
    slot_ids = jnp.arange(slot_total, dtype=jnp.int32)
    receiver_hot = (edge_receiver[:, None] == slot_ids[None, :]).astype(jnp.bfloat16)
    states = nodes
    edge_state = edges
    for layer_index in range(layer_count):
        first_weight = edge_w1[layer_index]
        near_out = jnp.take(states, near_flat, axis=0).reshape(span, near_width, features)
        near_in = []
        for offset_index in range(span):
            offset = offset_index - reach
            if offset == 0:
                near_in.append(near_out[offset_index])
            else:
                near_in.append(move_rows(near_out[offset_index], offset))
        outgoing = jnp.take(states, far_flat, axis=0).reshape(peer_count, slot_width, features)
        far_in = lax.all_to_all(outgoing, ("node", "feat"), split_axis=0, concat_axis=0, tiled=True)
        arrived = jnp.concatenate(
            [jnp.stack(near_in).reshape(near_total, features), far_in.reshape(far_total, features)],
            axis=0,
        )
        joined = jnp.concatenate(
            [
                edge_state,
                jnp.take(arrived, edge_sender, axis=0),
                jnp.take(arrived, edge_receiver, axis=0),
            ],
            axis=1,
        )
        pre_act = jnp.dot(joined, first_weight, preferred_element_type=jnp.float32)
        mixed_rows = second_half(pre_act, edge_b1[layer_index], edge_w2[layer_index])
        edge_state = finish(edge_state, mixed_rows, edge_gain[layer_index], edge_shift[layer_index])
        slot_sums = lax.dot_general(
            receiver_hot, edge_state, (((0,), (0,)), ((), ())), preferred_element_type=jnp.float32
        )
        near_sums = slot_sums[:near_total].reshape(span, near_width, features)
        near_back = []
        for offset_index in range(span):
            offset = offset_index - reach
            if offset == 0:
                near_back.append(near_sums[offset_index])
            else:
                near_back.append(return_sums(near_sums[offset_index], -offset))
        far_sums = slot_sums[near_total:].reshape(peer_count, slot_width, features)
        far_back = lax.all_to_all(
            far_sums.astype(jnp.bfloat16), ("node", "feat"), split_axis=0, concat_axis=0, tiled=True
        ).astype(far_sums.dtype)
        returned = jnp.concatenate(
            [
                jnp.stack(near_back).reshape(near_total, features),
                far_back.reshape(far_total, features),
            ],
            axis=0,
        )
        aggregate = jax.ops.segment_sum(returned, owner_rows, num_segments=node_rows)
        joined_nodes = jnp.concatenate([states, aggregate.astype(jnp.bfloat16)], axis=1)
        node_pre = jnp.dot(joined_nodes, node_w1[layer_index], preferred_element_type=jnp.float32)
        node_mixed = second_half(node_pre, node_b1[layer_index], node_w2[layer_index])
        states = finish(states, node_mixed, node_gain[layer_index], node_shift[layer_index])
    return (states, edge_state)


def solution(mesh):
    return jax.shard_map(
        on_device,
        mesh=mesh,
        in_specs=(
            P(("ens", "node", "feat"), None),
            P(("ens", "node", "feat"), None),
            P(("ens", "node", "feat"), None, None),
            P(("ens", "node", "feat"), None, None),
            P(("ens", "node", "feat")),
            P(("ens", "node", "feat")),
            P(),
            P(),
            P(),
            P(),
            P(),
            P(),
            P(),
            P(),
            P(),
            P(),
        ),
        out_specs=(P(("ens", "node", "feat"), None), P(("ens", "node", "feat"), None)),
        check_vma=False,
    )
```

profile of v0, /device:TPU:0, one launch (start us, length us, event | category | flops | bytes accessed | tf_op | source)
XLA Modules:
  0.0 170.1 jit_solution(13739660435400639900)
XLA Ops:
  0.7 0.9 copy.23
  1.6 0.1 reshape.155
  1.7 0.7 reduce
  2.4 0.1 reshape.154
  2.5 1.6 gather_fusion.1
  4.2 0.6 reshape.157
  4.8 7.4 %all-to-all-start = ((bf16[16,2,512]{2,1,0:T(2,128)(2,1)}), bf16[16,2,512]{2,1,0:T(2,128)(2,1)S(1)}, u32[]{:S(2)}, u32[]{:S(2)}) async-start(bf16[16,2,512]{2,1,0:T(2,128)(2,1)} %reshape.157), calls=%async_computation | async-start | bytes 65536 | tf_op jit(solution)/shard_map/all_to_all | solution.py:87
  12.2 2.1 %gather_fusion = bf16[240,512]{1,0:T(8,128)(2,1)S(1)} fusion(bf16[128,512]{1,0:T(8,128)(2,1)} %param.22, s32[1024]{0:T(1024)S(1)} %get-tuple-element.52), kind=kCustom, calls=%fused_computation.clone | custom fusion | bytes 492480 | tf_op jit(solution)/shard_map/jit(_take)/gather | solution.py:78
  14.3 0.1 broadcast_select_fusion.5
  14.4 2.0 %collective-permute-start.3 = (bf16[48,512]{1,0:T(8,128)(2,1)S(1)}, bf16[48,512]{1,0:T(8,128)(2,1)S(1)}, u32[]{:S(2)}, u32[]{:S(2)}) collective-permute-start(bf16[48,512]{1,0:T(8,128)(2,1)S(1)} %get-tuple-element.21), channel_id=1, source_target_pairs={{14,0},{15,1},{0,2},{1,3},{2,4},{3,5},{4,6},{5,7},{6,8},{7,9},{8,1... | collective-permute-start | bytes 147464 | tf_op jit(solution)/shard_map/ppermute | solution.py:12
  16.4 4.4 %collective-permute-start.1 = (bf16[48,512]{1,0:T(8,128)(2,1)S(1)}, bf16[48,512]{1,0:T(8,128)(2,1)S(1)}, u32[]{:S(2)}, u32[]{:S(2)}) collective-permute-start(bf16[48,512]{1,0:T(8,128)(2,1)S(1)} %get-tuple-element.23), channel_id=1, source_target_pairs={{1,0},{2,1},{3,2},{4,3},{5,4},{6,5},{7,6},{8,7},{9,8},{10,9},{11,1... | collective-permute-start | bytes 147464 | tf_op jit(solution)/shard_map/ppermute | solution.py:12
  20.8 0.1 collective-permute-start
  21.1 2.4 %copy.24 = bf16[2048,512]{0,1:T(8,128)(2,1)} copy(bf16[2048,512]{1,0:T(8,128)(2,1)S(1)} %copy-done.7) | data formatting | bytes 4194304 | tf_op args[1]
  23.5 1.4 collective-permute-done
  25.1 7.5 %gather_fusion.3 = bf16[2048,512]{1,0:T(8,128)(2,1)S(1)} fusion(bf16[272,512]{1,0:T(8,128)(2,1)S(1)} %pad_maximum_fusion, s32[2048]{0:T(1024)S(1)} %get-tuple-element.50), kind=kCustom, calls=%fused_computation.5.clone | custom fusion | bytes 4202496 | tf_op jit(solution)/shard_map/jit(_take)/gather | solution.py:96
  32.6 9.2 %gather_fusion.2 = bf16[2048,512]{1,0:T(8,128)(2,1)} fusion(bf16[272,512]{1,0:T(8,128)(2,1)S(1)} %pad_maximum_fusion, s32[2048]{0:T(1024)S(1)} %get-tuple-element.49), kind=kCustom, calls=%fused_computation.2.clone | custom fusion | bytes 4202496 | tf_op jit(solution)/shard_map/jit(_take)/gather | solution.py:95
  41.8 1.6 broadcast_select_fusion
  43.4 0.8 copy-done.3
  44.2 1.6 broadcast_select_fusion.1
  45.8 9.3 %fusion.115 = (f32[2048]{0:T(1024)S(1)}, f32[2048,512]{0,1:T(8,128)}) fusion(bf16[2,512,512]{2,1,0:T(8,128)(2,1)} %param.30, bf16[2048,512]{1,0:T(8,128)(2,1)} %broadcast_select_fusion, bf16[2048,512]{1,0:T(8,128)(2,1)} %broadcast_select_fusion.1, bf16[2048,512]{1,0:T(8,128)(2,1)} %param.23, f32[512]{0:T(512)S(1)} %bitcast.139, ...), kind=kOutput, calls=%fused_computation.155 | convolution fusion | flops 4321179648 | bytes 12593152 | tf_op jit(solution)/shard_map/dot_general | solution.py:29
  55.0 2.8 %multiply_reduce_fusion.1 = f32[2048]{0:T(1024)S(1)} fusion(f32[2048,512]{0,1:T(8,128)} %get-tuple-element.38, f32[2048]{0:T(1024)S(1)} %broadcast_multiply_fusion.1), kind=kLoop, calls=%fused_computation.26 | loop fusion | flops 3143680 | bytes 4210688 | tf_op jit(solution)/shard_map/reduce_sum | solution.py:17
  57.9 0.6 copy-done.2
  58.5 1.0 add_convert_fusion.1
  59.5 1.4 fusion.120
  61.0 0.6 collective-permute-start.4
  61.7 0.6 convert_element_type.73
  62.3 5.6 %all-to-all-start.1 = ((bf16[16,2,512]{2,1,0:T(2,128)(2,1)}), bf16[16,2,512]{2,1,0:T(2,128)(2,1)S(1)}, u32[]{:S(2)}, u32[]{:S(2)}) async-start(bf16[16,2,512]{2,1,0:T(2,128)(2,1)} %convert_element_type.73), calls=%async_computation.1 | async-start | bytes 65536 | tf_op jit(solution)/shard_map/all_to_all | solution.py:115
  67.9 4.6 %collective-permute-start.7 = (bf16[48,512]{1,0:T(8,128)(2,1)S(1)}, bf16[48,512]{1,0:T(8,128)(2,1)S(1)}, u32[]{:S(2)}, u32[]{:S(2)}) collective-permute-start(bf16[48,512]{1,0:T(8,128)(2,1)S(1)} %get-tuple-element.13), channel_id=1, source_target_pairs={{2,0},{3,1},{4,2},{5,3},{6,4},{7,5},{8,6},{9,7},{10,8},{11,9},{12,... | collective-permute-start | bytes 147464 | tf_op jit(solution)/shard_map/ppermute | solution.py:12
  72.6 0.5 collective-permute-start.5
  73.0 5.7 %collective-permute-done.5 = bf16[48,512]{1,0:T(8,128)(2,1)S(1)} collective-permute-done((bf16[48,512]{1,0:T(8,128)(2,1)S(1)}, bf16[48,512]{1,0:T(8,128)(2,1)S(1)}, u32[]{:S(2)}, u32[]{:S(2)}) %collective-permute-start.5) | collective-permute-done | bytes 49184 | tf_op jit(solution)/shard_map/ppermute | solution.py:12
  78.9 2.3 %scatter_custom_fusion = f32[128,512]{1,0:T(8,128)S(1)} fusion(s32[272]{0:T(512)S(1)} %pad_add_fusion, f32[32,512]{1,0:T(8,128)S(1)} %reshape.173, f32[]{:T(128)} %constant.58, f32[240,512]{1,0:T(8,128)S(1)} %bitcast.124, f32[]{:T(128)} %constant.42.clone.1), kind=kCustom, calls=%fused_computation.50 | custom fusion | flops 278528 | bytes 819208 | tf_op jit(solution)/shard_map/scatter-add | solution.py:125
  81.2 2.0 %fusion.121 = (f32[128]{0:T(128)S(1)}, f32[128,512]{1,0:T(8,128)S(1)}) fusion(bf16[2,512,512]{2,1,0:T(8,128)(2,1)} %param.35, bf16[2,1024,512]{2,1,0:T(8,128)(2,1)} %param.33, bf16[128,512]{1,0:T(8,128)(2,1)S(1)} %convert_element_type.74, bf16[128,512]{1,0:T(8,128)(2,1)S(1)} %copy-done, f32[512]{0:T(512)S(1)} %bitcast.138), kind=kOutput, calls=%fused_computation.157 | convolution fusion | flops 202309504 | bytes 2099712 | tf_op jit(solution)/shard_map/dot_general | solution.py:29
  83.2 0.2 multiply_reduce_fusion.3
  83.4 0.1 add_convert_fusion.3
  83.5 0.6 gather_fusion.5
  84.2 1.1 gather_fusion.4
  85.3 0.1 broadcast_select_fusion.4
  85.4 0.7 collective-permute-start.8
  86.2 0.6 reshape.163
  86.8 3.5 %all-to-all-start.2 = ((bf16[16,2,512]{2,1,0:T(2,128)(2,1)}), bf16[16,2,512]{2,1,0:T(2,128)(2,1)S(1)}, u32[]{:S(2)}, u32[]{:S(2)}) async-start(bf16[16,2,512]{2,1,0:T(2,128)(2,1)} %reshape.163), calls=%async_computation.2 | async-start | bytes 65536 | tf_op jit(solution)/shard_map/all_to_all | solution.py:87
  90.3 1.8 %collective-permute-start.11 = (bf16[48,512]{1,0:T(8,128)(2,1)S(1)}, bf16[48,512]{1,0:T(8,128)(2,1)S(1)}, u32[]{:S(2)}, u32[]{:S(2)}) collective-permute-start(bf16[48,512]{1,0:T(8,128)(2,1)S(1)} %get-tuple-element.17), channel_id=1, source_target_pairs={{14,0},{15,1},{0,2},{1,3},{2,4},{3,5},{4,6},{5,7},{6,8},{7,9},{8,1... | collective-permute-start | bytes 147464 | tf_op jit(solution)/shard_map/ppermute | solution.py:12
  92.2 4.4 %collective-permute-start.9 = (bf16[48,512]{1,0:T(8,128)(2,1)S(1)}, bf16[48,512]{1,0:T(8,128)(2,1)S(1)}, u32[]{:S(2)}, u32[]{:S(2)}) collective-permute-start(bf16[48,512]{1,0:T(8,128)(2,1)S(1)} %get-tuple-element.19), channel_id=1, source_target_pairs={{1,0},{2,1},{3,2},{4,3},{5,4},{6,5},{7,6},{8,7},{9,8},{10,9},{11,1... | collective-permute-start | bytes 147464 | tf_op jit(solution)/shard_map/ppermute | solution.py:12
  96.6 1.7 %collective-permute-done.9 = bf16[48,512]{1,0:T(8,128)(2,1)S(1)} collective-permute-done((bf16[48,512]{1,0:T(8,128)(2,1)S(1)}, bf16[48,512]{1,0:T(8,128)(2,1)S(1)}, u32[]{:S(2)}, u32[]{:S(2)}) %collective-permute-start.9) | collective-permute-done | bytes 49184 | tf_op jit(solution)/shard_map/ppermute | solution.py:12
  98.5 9.2 %gather_fusion.7 = bf16[2048,512]{1,0:T(8,128)(2,1)} fusion(bf16[272,512]{1,0:T(8,128)(2,1)S(1)} %pad_maximum_fusion.1, s32[2048]{0:T(1024)S(1)} %get-tuple-element.50), kind=kCustom, calls=%fused_computation.7.clone | custom fusion | bytes 4202496 | tf_op jit(solution)/shard_map/jit(_take)/gather | solution.py:96
  107.7 7.5 %gather_fusion.6 = bf16[2048,512]{1,0:T(8,128)(2,1)S(1)} fusion(bf16[272,512]{1,0:T(8,128)(2,1)S(1)} %pad_maximum_fusion.1, s32[2048]{0:T(1024)S(1)} %get-tuple-element.49), kind=kCustom, calls=%fused_computation.6.clone | custom fusion | bytes 4202496 | tf_op jit(solution)/shard_map/jit(_take)/gather | solution.py:95
  115.2 4.0 %copy.26 = bf16[2048,512]{0,1:T(8,128)(2,1)} copy(bf16[2048,512]{1,0:T(8,128)(2,1)} %gather_fusion.7) | data formatting | bytes 4194304 | tf_op jit(solution)/shard_map/jit(_take)/gather | solution.py:96
  119.2 3.1 %broadcast_select_fusion.2 = bf16[2048,512]{0,1:T(8,128)(2,1)} fusion(bf16[2048,512]{0,1:T(8,128)(2,1)} %copy.26, pred[2048]{0:T(1024)(128)(4,1)S(1)} %compare_and_fusion), kind=kLoop, calls=%fused_computation.34 | loop fusion | flops 1048576 | bytes 4196352 | tf_op jit(solution)/shard_map/jit(_take)/select_n | solution.py:96
  122.4 2.5 %copy.25 = bf16[2048,512]{0,1:T(8,128)(2,1)} copy(bf16[2048,512]{1,0:T(8,128)(2,1)S(1)} %gather_fusion.6) | data formatting | bytes 4194304 | tf_op jit(solution)/shard_map/jit(_take)/gather | solution.py:95
  124.9 3.3 %broadcast_select_fusion.3 = bf16[2048,512]{0,1:T(8,128)(2,1)} fusion(bf16[2048,512]{0,1:T(8,128)(2,1)} %copy.25, pred[2048]{0:T(1024)(128)(4,1)S(1)} %compare_and_fusion.1), kind=kLoop, calls=%fused_computation.35 | loop fusion | flops 1048576 | bytes 4196352 | tf_op jit(solution)/shard_map/jit(_take)/select_n | solution.py:95
  128.2 8.9 %fusion.126 = (f32[2048]{0:T(1024)S(1)}, f32[2048,512]{0,1:T(8,128)}) fusion(bf16[2,512,512]{2,1,0:T(8,128)(2,1)} %param.30, bf16[2048,512]{0,1:T(8,128)(2,1)} %broadcast_select_fusion.2, bf16[2048,512]{0,1:T(8,128)(2,1)} %broadcast_select_fusion.3, bf16[2048,512]{0,1:T(8,128)(2,1)S(1)} %copy-done.6, f32[512]{0:T(512)S(1)} %bitcast.137, ...), kind=kOutput, calls=%fused_computation.158 | convolution fusion | flops 4321179648 | bytes 12593152 | tf_op jit(solution)/shard_map/dot_general | solution.py:29
  137.1 2.8 %multiply_reduce_fusion = f32[2048]{0:T(1024)S(1)} fusion(f32[2048,512]{0,1:T(8,128)} %get-tuple-element.44, f32[2048]{0:T(1024)S(1)} %broadcast_multiply_fusion), kind=kLoop, calls=%fused_computation.23 | loop fusion | flops 3143680 | bytes 4210688 | tf_op jit(solution)/shard_map/reduce_sum | solution.py:17
  139.9 0.6 copy-done.1
  140.6 2.6 %add_convert_fusion = bf16[2048,512]{0,1:T(8,128)(2,1)S(1)} fusion(bf16[2048,512]{0,1:T(8,128)(2,1)} %copy-done.5, f32[2048,512]{0,1:T(8,128)S(1)} %copy-done.1, f32[512]{0:T(512)S(1)} %bitcast.133, f32[512]{0:T(512)S(1)} %bitcast.132, f32[2048]{0:T(1024)S(1)} %add_rsqrt_fusion, f32[2048]{0:T(1024)S(1)} %broadcast_multiply_fusion), kind=kLoop, calls=%fused_computation.22 | loop fusion | flops 7340032 | bytes 8409088 | tf_op jit(solution)/shard_map/convert_element_type | solution.py:22
  143.2 1.4 fusion.131
  144.6 2.5 %copy.27 = bf16[2048,512]{1,0:T(8,128)(2,1)} copy(bf16[2048,512]{0,1:T(8,128)(2,1)S(1)} %add_convert_fusion) | data formatting | bytes 4194304
  147.2 0.6 convert_element_type.81
  147.8 6.1 %all-to-all-start.3 = ((bf16[16,2,512]{2,1,0:T(2,128)(2,1)}), bf16[16,2,512]{2,1,0:T(2,128)(2,1)S(1)}, u32[]{:S(2)}, u32[]{:S(2)}) async-start(bf16[16,2,512]{2,1,0:T(2,128)(2,1)} %convert_element_type.81), calls=%async_computation.3 | async-start | bytes 65536 | tf_op jit(solution)/shard_map/all_to_all | solution.py:115
  153.9 4.6 %collective-permute-start.15 = (bf16[48,512]{1,0:T(8,128)(2,1)S(1)}, bf16[48,512]{1,0:T(8,128)(2,1)S(1)}, u32[]{:S(2)}, u32[]{:S(2)}) collective-permute-start(bf16[48,512]{1,0:T(8,128)(2,1)S(1)} %get-tuple-element.9), channel_id=1, source_target_pairs={{2,0},{3,1},{4,2},{5,3},{6,4},{7,5},{8,6},{9,7},{10,8},{11,9},{12,... | collective-permute-start | bytes 147464 | tf_op jit(solution)/shard_map/ppermute | solution.py:12
  158.6 0.5 collective-permute-start.13
  159.0 5.7 %collective-permute-done.13 = bf16[48,512]{1,0:T(8,128)(2,1)S(1)} collective-permute-done((bf16[48,512]{1,0:T(8,128)(2,1)S(1)}, bf16[48,512]{1,0:T(8,128)(2,1)S(1)}, u32[]{:S(2)}, u32[]{:S(2)}) %collective-permute-start.13) | collective-permute-done | bytes 49184 | tf_op jit(solution)/shard_map/ppermute | solution.py:12
  164.9 2.3 %scatter_custom_fusion.1 = f32[128,512]{1,0:T(8,128)S(1)} fusion(s32[272]{0:T(512)S(1)} %pad_add_fusion, f32[32,512]{1,0:T(8,128)S(1)} %reshape.179, f32[]{:T(128)} %constant.58, f32[240,512]{1,0:T(8,128)S(1)} %bitcast.125, f32[]{:T(128)} %constant.42.clone.1), kind=kCustom, calls=%fused_computation.54 | custom fusion | flops 278528 | bytes 819208 | tf_op jit(solution)/shard_map/scatter-add | solution.py:125
  167.2 1.8 %fusion.132 = (f32[128]{0:T(128)S(1)}, f32[128,512]{1,0:T(8,128)S(1)}) fusion(bf16[2,512,512]{2,1,0:T(8,128)(2,1)S(1)} %copy-done.16, bf16[2,1024,512]{2,1,0:T(8,128)(2,1)} %param.33, bf16[128,512]{1,0:T(8,128)(2,1)S(1)} %convert_element_type.82, bf16[128,512]{1,0:T(8,128)(2,1)S(1)} %add_convert_fusion.3, f32[512]{0:T(512)S(1)} %bitcast.136), kind=kOutput, calls=%fused_computation.160 | convolution fusion | flops 202309504 | bytes 2099712 | tf_op jit(solution)/shard_map/dot_general | solution.py:29
  169.0 0.2 multiply_reduce_fusion.2
  169.2 0.8 add_convert_fusion.2
  (111 shorter events, 1.0 us)
Async XLA Ops:
  0.6 20.3 %copy-start.8 = (s32[2048]{0:T(1024)S(1)}, s32[2048]{0:T(1024)}, u32[]{:S(2)}) copy-start(s32[2048]{0:T(1024)} %param.26) | copy-start | bytes 24580
  0.6 20.3 %copy-start.9 = (s32[2048]{0:T(1024)S(1)}, s32[2048]{0:T(1024)}, u32[]{:S(2)}) copy-start(s32[2048]{0:T(1024)} %param.27) | copy-start | bytes 24580
  0.7 20.3 %copy-start.10 = (f32[2,512]{1,0:T(2,128)S(1)}, f32[2,512]{1,0:T(2,128)}, u32[]{:S(2)}) copy-start(f32[2,512]{1,0:T(2,128)} %param.29) | copy-start | bytes 12292
  0.7 20.4 %copy-start.11 = (f32[2,512]{1,0:T(2,128)S(1)}, f32[2,512]{1,0:T(2,128)}, u32[]{:S(2)}) copy-start(f32[2,512]{1,0:T(2,128)} %param.31) | copy-start | bytes 12292
  0.7 20.4 %copy-start.12 = (f32[2,512]{1,0:T(2,128)S(1)}, f32[2,512]{1,0:T(2,128)}, u32[]{:S(2)}) copy-start(f32[2,512]{1,0:T(2,128)} %param.32) | copy-start | bytes 12292
  0.7 20.4 %copy-start.13 = (f32[2,512]{1,0:T(2,128)S(1)}, f32[2,512]{1,0:T(2,128)}, u32[]{:S(2)}) copy-start(f32[2,512]{1,0:T(2,128)} %param.34) | copy-start | bytes 12292
  0.7 20.4 %copy-start.14 = (f32[2,512]{1,0:T(2,128)S(1)}, f32[2,512]{1,0:T(2,128)}, u32[]{:S(2)}) copy-start(f32[2,512]{1,0:T(2,128)} %param.36) | copy-start | bytes 12292
  0.7 20.4 %copy-start.15 = (f32[2,512]{1,0:T(2,128)S(1)}, f32[2,512]{1,0:T(2,128)}, u32[]{:S(2)}) copy-start(f32[2,512]{1,0:T(2,128)} %param.37) | copy-start | bytes 12292
  0.7 20.4 %copy-start.7 = (bf16[2048,512]{1,0:T(8,128)(2,1)S(1)}, bf16[2048,512]{1,0:T(8,128)(2,1)}, u32[]{:S(2)}) copy-start(bf16[2048,512]{1,0:T(8,128)(2,1)} %param.23) | copy-start | bytes 6291460
  4.8 20.2 %all-to-all-start = ((bf16[16,2,512]{2,1,0:T(2,128)(2,1)}), bf16[16,2,512]{2,1,0:T(2,128)(2,1)S(1)}, u32[]{:S(2)}, u32[]{:S(2)}) async-start(bf16[16,2,512]{2,1,0:T(2,128)(2,1)} %reshape.157), calls=%async_computation | async-start | bytes 65536 | tf_op jit(solution)/shard_map/all_to_all | solution.py:87
  14.4 10.6 %collective-permute-start.3 = (bf16[48,512]{1,0:T(8,128)(2,1)S(1)}, bf16[48,512]{1,0:T(8,128)(2,1)S(1)}, u32[]{:S(2)}, u32[]{:S(2)}) collective-permute-start(bf16[48,512]{1,0:T(8,128)(2,1)S(1)} %get-tuple-element.21), channel_id=1, source_target_pairs={{14,0},{15,1},{0,2},{1,3},{2,4},{3,5},{4,6},{5,7},{6,8},{7,9},{8,1... | collective-permute-start | bytes 147464 | tf_op jit(solution)/shard_map/ppermute | solution.py:12
  16.4 8.6 %collective-permute-start.2 = (bf16[48,512]{1,0:T(8,128)(2,1)S(1)}, bf16[48,512]{1,0:T(8,128)(2,1)S(1)}, u32[]{:S(2)}, u32[]{:S(2)}) collective-permute-start(bf16[48,512]{1,0:T(8,128)(2,1)S(1)} %get-tuple-element.22), channel_id=1, source_target_pairs={{15,0},{0,1},{1,2},{2,3},{3,4},{4,5},{5,6},{6,7},{7,8},{8,9},{9,10... | collective-permute-start | bytes 147464 | tf_op jit(solution)/shard_map/ppermute | solution.py:12
  16.4 8.5 %collective-permute-start.1 = (bf16[48,512]{1,0:T(8,128)(2,1)S(1)}, bf16[48,512]{1,0:T(8,128)(2,1)S(1)}, u32[]{:S(2)}, u32[]{:S(2)}) collective-permute-start(bf16[48,512]{1,0:T(8,128)(2,1)S(1)} %get-tuple-element.23), channel_id=1, source_target_pairs={{1,0},{2,1},{3,2},{4,3},{5,4},{6,5},{7,6},{8,7},{9,8},{10,9},{11,1... | collective-permute-start | bytes 147464 | tf_op jit(solution)/shard_map/ppermute | solution.py:12
  20.8 4.1 %collective-permute-start = (bf16[48,512]{1,0:T(8,128)(2,1)S(1)}, bf16[48,512]{1,0:T(8,128)(2,1)S(1)}, u32[]{:S(2)}, u32[]{:S(2)}) collective-permute-start(bf16[48,512]{1,0:T(8,128)(2,1)S(1)} %get-tuple-element.24), channel_id=1, source_target_pairs={{2,0},{3,1},{4,2},{5,3},{6,4},{7,5},{8,6},{9,7},{10,8},{11,9},{12,... | collective-permute-start | bytes 147464 | tf_op jit(solution)/shard_map/ppermute | solution.py:12
  41.8 2.3 %copy-start.3 = (bf16[2048,512]{1,0:T(8,128)(2,1)S(1)}, bf16[2048,512]{1,0:T(8,128)(2,1)}, u32[]{:S(2)}) copy-start(bf16[2048,512]{1,0:T(8,128)(2,1)} %gather_fusion.2) | copy-start | bytes 6291460
  45.8 12.1 %copy-start.4 = (bf16[2048,512]{0,1:T(8,128)(2,1)S(1)}, bf16[2048,512]{0,1:T(8,128)(2,1)}, u32[]{:S(2)}) copy-start(bf16[2048,512]{0,1:T(8,128)(2,1)} %copy.24) | copy-start | bytes 6291460
  55.0 3.4 %copy-start.2 = (f32[2048,512]{0,1:T(8,128)S(1)}, f32[2048,512]{0,1:T(8,128)}, u32[]{:S(2)}) copy-start(f32[2048,512]{0,1:T(8,128)} %get-tuple-element.38) | copy-start | bytes 12582916
  59.5 1.4 copy-start.5
  61.0 20.2 %copy-start = (bf16[128,512]{1,0:T(8,128)(2,1)S(1)}, bf16[128,512]{1,0:T(8,128)(2,1)}, u32[]{:S(2)}) copy-start(bf16[128,512]{1,0:T(8,128)(2,1)} %param.22) | copy-start | bytes 393220
  61.0 12.0 %collective-permute-start.4 = (bf16[48,512]{1,0:T(8,128)(2,1)S(1)}, bf16[48,512]{1,0:T(8,128)(2,1)S(1)}, u32[]{:S(2)}, u32[]{:S(2)}) collective-permute-start(bf16[48,512]{1,0:T(8,128)(2,1)S(1)} %get-tuple-element.16), channel_id=1, source_target_pairs={{14,0},{15,1},{0,2},{1,3},{2,4},{3,5},{4,6},{5,7},{6,8},{7,9},{8,1... | collective-permute-start | bytes 147464 | tf_op jit(solution)/shard_map/ppermute | solution.py:12
  62.3 16.6 %all-to-all-start.1 = ((bf16[16,2,512]{2,1,0:T(2,128)(2,1)}), bf16[16,2,512]{2,1,0:T(2,128)(2,1)S(1)}, u32[]{:S(2)}, u32[]{:S(2)}) async-start(bf16[16,2,512]{2,1,0:T(2,128)(2,1)} %convert_element_type.73), calls=%async_computation.1 | async-start | bytes 65536 | tf_op jit(solution)/shard_map/all_to_all | solution.py:115
  67.9 11.0 %collective-permute-start.7 = (bf16[48,512]{1,0:T(8,128)(2,1)S(1)}, bf16[48,512]{1,0:T(8,128)(2,1)S(1)}, u32[]{:S(2)}, u32[]{:S(2)}) collective-permute-start(bf16[48,512]{1,0:T(8,128)(2,1)S(1)} %get-tuple-element.13), channel_id=1, source_target_pairs={{2,0},{3,1},{4,2},{5,3},{6,4},{7,5},{8,6},{9,7},{10,8},{11,9},{12,... | collective-permute-start | bytes 147464 | tf_op jit(solution)/shard_map/ppermute | solution.py:12
  72.5 6.3 %collective-permute-start.6 = (bf16[48,512]{1,0:T(8,128)(2,1)S(1)}, bf16[48,512]{1,0:T(8,128)(2,1)S(1)}, u32[]{:S(2)}, u32[]{:S(2)}) collective-permute-start(bf16[48,512]{1,0:T(8,128)(2,1)S(1)} %get-tuple-element.14), channel_id=1, source_target_pairs={{1,0},{2,1},{3,2},{4,3},{5,4},{6,5},{7,6},{8,7},{9,8},{10,9},{11,1... | collective-permute-start | bytes 147464 | tf_op jit(solution)/shard_map/ppermute | solution.py:12
  72.6 6.2 %collective-permute-start.5 = (bf16[48,512]{1,0:T(8,128)(2,1)S(1)}, bf16[48,512]{1,0:T(8,128)(2,1)S(1)}, u32[]{:S(2)}, u32[]{:S(2)}) collective-permute-start(bf16[48,512]{1,0:T(8,128)(2,1)S(1)} %get-tuple-element.15), channel_id=1, source_target_pairs={{15,0},{0,1},{1,2},{2,3},{3,4},{4,5},{5,6},{6,7},{7,8},{8,9},{9,10... | collective-permute-start | bytes 147464 | tf_op jit(solution)/shard_map/ppermute | solution.py:12
  85.4 11.2 %collective-permute-start.8 = (bf16[48,512]{1,0:T(8,128)(2,1)S(1)}, bf16[48,512]{1,0:T(8,128)(2,1)S(1)}, u32[]{:S(2)}, u32[]{:S(2)}) collective-permute-start(bf16[48,512]{1,0:T(8,128)(2,1)S(1)} %get-tuple-element.20), channel_id=1, source_target_pairs={{2,0},{3,1},{4,2},{5,3},{6,4},{7,5},{8,6},{9,7},{10,8},{11,9},{12,... | collective-permute-start | bytes 147464 | tf_op jit(solution)/shard_map/ppermute | solution.py:12
  86.8 11.6 %all-to-all-start.2 = ((bf16[16,2,512]{2,1,0:T(2,128)(2,1)}), bf16[16,2,512]{2,1,0:T(2,128)(2,1)S(1)}, u32[]{:S(2)}, u32[]{:S(2)}) async-start(bf16[16,2,512]{2,1,0:T(2,128)(2,1)} %reshape.163), calls=%async_computation.2 | async-start | bytes 65536 | tf_op jit(solution)/shard_map/all_to_all | solution.py:87
  90.3 8.1 %collective-permute-start.11 = (bf16[48,512]{1,0:T(8,128)(2,1)S(1)}, bf16[48,512]{1,0:T(8,128)(2,1)S(1)}, u32[]{:S(2)}, u32[]{:S(2)}) collective-permute-start(bf16[48,512]{1,0:T(8,128)(2,1)S(1)} %get-tuple-element.17), channel_id=1, source_target_pairs={{14,0},{15,1},{0,2},{1,3},{2,4},{3,5},{4,6},{5,7},{6,8},{7,9},{8,1... | collective-permute-start | bytes 147464 | tf_op jit(solution)/shard_map/ppermute | solution.py:12
  92.1 6.3 %collective-permute-start.10 = (bf16[48,512]{1,0:T(8,128)(2,1)S(1)}, bf16[48,512]{1,0:T(8,128)(2,1)S(1)}, u32[]{:S(2)}, u32[]{:S(2)}) collective-permute-start(bf16[48,512]{1,0:T(8,128)(2,1)S(1)} %get-tuple-element.18), channel_id=1, source_target_pairs={{15,0},{0,1},{1,2},{2,3},{3,4},{4,5},{5,6},{6,7},{7,8},{8,9},{9,10... | collective-permute-start | bytes 147464 | tf_op jit(solution)/shard_map/ppermute | solution.py:12
  92.2 6.2 %collective-permute-start.9 = (bf16[48,512]{1,0:T(8,128)(2,1)S(1)}, bf16[48,512]{1,0:T(8,128)(2,1)S(1)}, u32[]{:S(2)}, u32[]{:S(2)}) collective-permute-start(bf16[48,512]{1,0:T(8,128)(2,1)S(1)} %get-tuple-element.19), channel_id=1, source_target_pairs={{1,0},{2,1},{3,2},{4,3},{5,4},{6,5},{7,6},{8,7},{9,8},{10,9},{11,1... | collective-permute-start | bytes 147464 | tf_op jit(solution)/shard_map/ppermute | solution.py:12
  124.9 3.3 %copy-start.6 = (bf16[2048,512]{0,1:T(8,128)(2,1)S(1)}, bf16[2048,512]{0,1:T(8,128)(2,1)}, u32[]{:S(2)}) copy-start(bf16[2048,512]{0,1:T(8,128)(2,1)} %copy-done.5) | copy-start | bytes 6291460
  137.1 3.4 %copy-start.1 = (f32[2048,512]{0,1:T(8,128)S(1)}, f32[2048,512]{0,1:T(8,128)}, u32[]{:S(2)}) copy-start(f32[2048,512]{0,1:T(8,128)} %get-tuple-element.44) | copy-start | bytes 12582916
  144.6 14.4 %collective-permute-start.12 = (bf16[48,512]{1,0:T(8,128)(2,1)S(1)}, bf16[48,512]{1,0:T(8,128)(2,1)S(1)}, u32[]{:S(2)}, u32[]{:S(2)}) collective-permute-start(bf16[48,512]{1,0:T(8,128)(2,1)S(1)} %get-tuple-element.12), channel_id=1, source_target_pairs={{14,0},{15,1},{0,2},{1,3},{2,4},{3,5},{4,6},{5,7},{6,8},{7,9},{8,1... | collective-permute-start | bytes 147464 | tf_op jit(solution)/shard_map/ppermute | solution.py:12
  147.1 20.1 %copy-start.16 = (bf16[2,512,512]{2,1,0:T(8,128)(2,1)S(1)}, bf16[2,512,512]{2,1,0:T(8,128)(2,1)}, u32[]{:S(2)}) copy-start(bf16[2,512,512]{2,1,0:T(8,128)(2,1)} %param.35) | copy-start | bytes 3145732
  147.8 17.1 %all-to-all-start.3 = ((bf16[16,2,512]{2,1,0:T(2,128)(2,1)}), bf16[16,2,512]{2,1,0:T(2,128)(2,1)S(1)}, u32[]{:S(2)}, u32[]{:S(2)}) async-start(bf16[16,2,512]{2,1,0:T(2,128)(2,1)} %convert_element_type.81), calls=%async_computation.3 | async-start | bytes 65536 | tf_op jit(solution)/shard_map/all_to_all | solution.py:115
  153.9 11.0 %collective-permute-start.15 = (bf16[48,512]{1,0:T(8,128)(2,1)S(1)}, bf16[48,512]{1,0:T(8,128)(2,1)S(1)}, u32[]{:S(2)}, u32[]{:S(2)}) collective-permute-start(bf16[48,512]{1,0:T(8,128)(2,1)S(1)} %get-tuple-element.9), channel_id=1, source_target_pairs={{2,0},{3,1},{4,2},{5,3},{6,4},{7,5},{8,6},{9,7},{10,8},{11,9},{12,... | collective-permute-start | bytes 147464 | tf_op jit(solution)/shard_map/ppermute | solution.py:12
  158.5 6.3 %collective-permute-start.14 = (bf16[48,512]{1,0:T(8,128)(2,1)S(1)}, bf16[48,512]{1,0:T(8,128)(2,1)S(1)}, u32[]{:S(2)}, u32[]{:S(2)}) collective-permute-start(bf16[48,512]{1,0:T(8,128)(2,1)S(1)} %get-tuple-element.10), channel_id=1, source_target_pairs={{1,0},{2,1},{3,2},{4,3},{5,4},{6,5},{7,6},{8,7},{9,8},{10,9},{11,1... | collective-permute-start | bytes 147464 | tf_op jit(solution)/shard_map/ppermute | solution.py:12
  158.6 6.2 %collective-permute-start.13 = (bf16[48,512]{1,0:T(8,128)(2,1)S(1)}, bf16[48,512]{1,0:T(8,128)(2,1)S(1)}, u32[]{:S(2)}, u32[]{:S(2)}) collective-permute-start(bf16[48,512]{1,0:T(8,128)(2,1)S(1)} %get-tuple-element.11), channel_id=1, source_target_pairs={{15,0},{0,1},{1,2},{2,3},{3,4},{4,5},{5,6},{6,7},{7,8},{8,9},{9,10... | collective-permute-start | bytes 147464 | tf_op jit(solution)/shard_map/ppermute | solution.py:12
where the time goes:
time: 171 us; the launch traced here: 170 us
  local copies, waits for them, and re-layouts  56.2 us (33%)
  starting transfers between devices  46.9 us (27%)
  other arithmetic  26.1 us (15%)
  matrix products  24.7 us (14%)
  waiting for transfers between devices  14.7 us (9%)
    ppermute x16, starting transfers between devices, passed_along(): return lax.ppermute(block, axis, route)  24.4 us
    dot_general x4, matrix products, second_half(): return jnp.dot(hidden, second_weight, preferred_element_type=jnp.float32)  21.9 us
    gather x3, local copies, waits for them, and re-layouts, on_device(): jnp.take(arrived, edge_receiver, axis=0)  20.7 us
    gather x3, local copies, waits for them, and re-layouts, on_device(): jnp.take(arrived, edge_sender, axis=0)  19.2 us
    ppermute x16, waiting for transfers between devices, passed_along(): return lax.ppermute(block, axis, route)  14.7 us
    all_to_all x2, starting transfers between devices, on_device(): lax.all_to_all(far_sums.astype(jnp.bfloat16), ('node', 'feat'), split_axi...  11.7 us
    all_to_all x2, starting transfers between devices, on_device(): lax.all_to_all(outgoing, ('node', 'feat'), split_axis=0, concat_axis=0, t...  10.9 us
    unnamed x47, local copies, waits for them, and re-layouts  7.97 us
  transfers between devices with their start and end apart: 20, of which 5 were waited for; matrix products, arithmetic and copies ran while one was open for 6% of the time, Pallas kernels for 0%

commit v1 on v0

v1 whole, which is shorter than its diff:
```python
import functools

import jax
import jax.numpy as jnp
from jax import lax
from jax.experimental import pallas as pl
from jax.experimental.pallas import tpu as pltpu
from jax.sharding import PartitionSpec as P

EPSILON = 1e-05
LANES = 128
BLOCK = 256
AXES = ("ens", "node", "feat")
MESH = pl.DeviceIdType.MESH


def round_up(value, multiple):
    return -(-value // multiple) * multiple


def dot(a, b):
    return jnp.dot(a, b, preferred_element_type=jnp.float32)


def layer_norm(values, norm_gain, norm_shift):
    center = values - jnp.mean(values, axis=-1, keepdims=True)
    spread = jnp.mean(center * center, axis=-1, keepdims=True)
    return center * lax.rsqrt(spread + EPSILON) * norm_gain + norm_shift


def gated(half):
    return (half + half * jnp.tanh(half)).astype(jnp.bfloat16)


def kernel(
    sizes,
    nodes, owner, senders, receivers,
    edge_b1, edge_gain, edge_shift, node_b1, node_gain, node_shift,
    edges_hbm, edge_w1_hbm, edge_w2_hbm, node_w1_hbm, node_w2_hbm,
    node_out, edge_out,
    edge_w1, edge_w2, node_w1, node_w2,
    states, edges, partial, hot, hot_t, owner_t, projected, sums,
    near_out, near_in, near_back_out, near_back_in,
    far_out, far_in, far_back_out, far_back_in,
    load_sems, store_sems,
    near_send, near_recv, far_send, far_recv,
):
    peers, feat_size, layers, span, near_width, cap, slots = sizes
    reach = (span - 1) // 2
    near_total = span * near_width
    padded = owner_t.shape[1]
    features = states.shape[1]
    columns = features // LANES
    edge_count = edges.shape[0]
    blocks = edge_count // BLOCK
    ens = lax.axis_index("ens")
    me = lax.axis_index("node") * feat_size + lax.axis_index("feat")

    def device(index):
        return (ens, index // feat_size, index % feat_size)

    loads = [pltpu.make_async_copy(edges_hbm, edges, load_sems.at[0])]
    for layer in range(layers):
        for place, (source, target) in enumerate(
            ((edge_w1_hbm, edge_w1), (edge_w2_hbm, edge_w2), (node_w1_hbm, node_w1), (node_w2_hbm, node_w2))
        ):
            loads.append(
                pltpu.make_async_copy(source.at[layer], target.at[layer], load_sems.at[1 + 4 * layer + place])
            )
    for load in loads:
        load.start()

    barrier = pltpu.get_barrier_semaphore()

    def greet(step, carry):
        pl.semaphore_signal(barrier, inc=1, device_id=device((me + step) % peers), device_id_type=MESH)
        return carry

    lax.fori_loop(1, peers, greet, 0)

    node_rows = states.shape[0]
    row_ids = lax.broadcasted_iota(jnp.int32, (node_rows, LANES), 0)
    for j in range(padded // LANES):
        picked = owner[:, j * LANES : (j + 1) * LANES] == row_ids
        owner_t[:, j * LANES : (j + 1) * LANES] = jnp.where(picked, 1.0, 0.0)

    states[...] = nodes[...]

    def near_copy(way, layer, k):
        source, target = ((near_out, near_in), (near_back_out, near_back_in))[way]
        rows = pl.ds(k * near_width, near_width)
        shift = (k - reach) if way == 0 else (reach - k)
        slot = (way * layers + layer) * span + k
        return pltpu.make_async_remote_copy(
            src_ref=source.at[layer, rows],
            dst_ref=target.at[layer, rows],
            send_sem=near_send.at[slot],
            recv_sem=near_recv.at[slot],
            device_id=device((me + shift + peers) % peers),
            device_id_type=MESH,
        )

    def far_copy(way, layer, step):
        source, target = ((far_out, far_in), (far_back_out, far_back_in))[way]
        to = (me + step) % peers
        slot = (way * layers + layer) * peers + step
        return pltpu.make_async_remote_copy(
            src_ref=source.at[layer, to],
            dst_ref=target.at[layer, me],
            send_sem=far_send.at[slot],
            recv_sem=far_recv.at[slot],
            device_id=device(to),
            device_id_type=MESH,
        )

    def far_arrival(way, layer, step):
        source, target = ((far_out, far_in), (far_back_out, far_back_in))[way]
        origin = (me + peers - step) % peers
        slot = (way * layers + layer) * peers + step
        return pltpu.make_async_remote_copy(
            src_ref=source.at[layer, origin],
            dst_ref=target.at[layer, origin],
            send_sem=far_send.at[slot],
            recv_sem=far_recv.at[slot],
            device_id=device(origin),
            device_id_type=MESH,
        )

    def send(way, layer, rows, first=False):
        source, far_source = ((near_out, far_out), (near_back_out, far_back_out))[way]
        target, far_target = ((near_in, far_in), (near_back_in, far_back_in))[way]
        source[layer, :near_total, :] = rows[:near_total].astype(jnp.bfloat16)
        for s in range(cap):
            begin = near_total + s * peers
            for c in range(columns):
                far_source[layer, :, s * columns + c, :] = rows[begin : begin + peers, c * LANES : (c + 1) * LANES]
        if first:
            pl.semaphore_wait(barrier, peers - 1)
        for k in range(span):
            if k != reach:
                near_copy(way, layer, k).start()

        def start(step, carry):
            far_copy(way, layer, step).start()
            return carry

        lax.fori_loop(1, peers, start, 0)
        own = slice(reach * near_width, (reach + 1) * near_width)
        target[layer, own, :] = source[layer, own, :]
        far_target[layer, pl.ds(me, 1)] = far_source[layer, pl.ds(me, 1)]
        target[layer, slots:, :] = jnp.zeros((padded - slots, features), jnp.bfloat16)

    def receive(way, layer):
        target, far_target = ((near_in, far_in), (near_back_in, far_back_in))[way]
        for k in range(span):
            if k != reach:
                near_copy(way, layer, k).wait_recv()

        def wait(step, carry):
            far_arrival(way, layer, step).wait_recv()
            return carry

        lax.fori_loop(1, peers, wait, 0)
        for s in range(cap):
            begin = near_total + s * peers
            for c in range(columns):
                target[layer, begin : begin + peers, c * LANES : (c + 1) * LANES] = far_target[
                    layer, :, s * columns + c, :
                ].astype(jnp.bfloat16)

    def gathered():
        pick = jnp.transpose(owner_t[...]).astype(jnp.bfloat16)
        return dot(pick, states[...])

    send(0, 0, gathered(), first=True)

    def renumbered(index):
        value = index.astype(jnp.float32)
        far = value - near_total
        peer = jnp.floor((far + 0.5) * (1.0 / cap))
        return jnp.where(value < near_total, value, near_total + (far - peer * cap) * peers + peer)

    sender_ids = renumbered(senders[...])
    receiver_ids = renumbered(receivers[...])
    lane_ids = lax.broadcasted_iota(jnp.int32, (LANES, LANES), 1).astype(jnp.float32)
    slot_ids = lax.broadcasted_iota(jnp.int32, (hot_t.shape[1], LANES), 0).astype(jnp.float32)
    for b in range(edge_count // LANES):
        rows = slice(b * LANES, (b + 1) * LANES)
        for side, ids in enumerate((sender_ids, receiver_ids)):
            column = jnp.transpose(jnp.broadcast_to(ids[b : b + 1], (LANES, LANES)))
            for j in range(padded // LANES):
                begin = side * padded + j * LANES
                hot[rows, begin : begin + LANES] = jnp.where(column == lane_ids + j * LANES, 1.0, 0.0).astype(
                    jnp.bfloat16
                )
        begin = (b * LANES) % BLOCK
        hot_t[b * LANES // BLOCK, :, begin : begin + LANES] = jnp.where(
            receiver_ids[b : b + 1] == slot_ids, 1.0, 0.0
        ).astype(jnp.bfloat16)

    loads[0].wait()
    for layer in range(layers):
        for place in range(4):
            if layer == 0 and place == 0:
                loads[1].wait()

        def own_term(i, carry, layer=layer):
            rows = pl.ds(pl.multiple_of(i * BLOCK, BLOCK), BLOCK)
            partial[rows, :] = 0.5 * (
                dot(edges[rows, :], edge_w1[layer, :features, :]) + edge_b1[layer : layer + 1, :]
            )
            return carry

        if layer == 0:
            lax.fori_loop(0, blocks, own_term, 0)
            for load in loads[2:]:
                load.wait()

        receive(0, layer)
        arrived = near_in[layer]
        for side in range(2):
            begin = (1 + side) * features
            projected[side * padded : (side + 1) * padded, :] = (
                0.5 * dot(arrived, edge_w1[layer, begin : begin + features, :])
            ).astype(jnp.bfloat16)

        sums[...] = jnp.zeros_like(sums)

        def update(i, carry, layer=layer):
            rows = pl.ds(pl.multiple_of(i * BLOCK, BLOCK), BLOCK)
            half = partial[rows, :] + dot(hot[rows, :], projected[...])
            mixed = dot(gated(half), edge_w2[layer])
            fresh = edges[rows, :].astype(jnp.float32) + layer_norm(
                mixed, edge_gain[layer : layer + 1, :], edge_shift[layer : layer + 1, :]
            )
            fresh = fresh.astype(jnp.bfloat16)
            edges[rows, :] = fresh
            if layer == layers - 1:
                pltpu.make_async_copy(edges.at[rows], edge_out.at[rows], store_sems.at[i]).start()
            sums[...] += dot(hot_t[i], fresh)
            return carry

        lax.fori_loop(0, blocks, update, 0)

        send(1, layer, sums)
        pre = dot(states[...], node_w1[layer, :features, :]) + node_b1[layer : layer + 1, :]
        if layer + 1 < layers:
            lax.fori_loop(0, blocks, functools.partial(own_term, layer=layer + 1), 0)
        receive(1, layer)
        aggregate = dot(owner_t[...].astype(jnp.bfloat16), near_back_in[layer]).astype(jnp.bfloat16)
        half = 0.5 * (pre + dot(aggregate, node_w1[layer, features:, :]))
        mixed = dot(gated(half), node_w2[layer])
        fresh = states[...].astype(jnp.float32) + layer_norm(
            mixed, node_gain[layer : layer + 1, :], node_shift[layer : layer + 1, :]
        )
        states[...] = fresh.astype(jnp.bfloat16)
        if layer + 1 < layers:
            send(0, layer + 1, gathered())

    node_out[...] = states[...]

    def drain(i, carry):
        rows = pl.ds(pl.multiple_of(i * BLOCK, BLOCK), BLOCK)
        pltpu.make_async_copy(edges.at[rows], edge_out.at[rows], store_sems.at[i]).wait()
        return carry

    lax.fori_loop(0, blocks, drain, 0)
    for way in range(2):
        for layer in range(layers):
            for k in range(span):
                if k != reach:
                    near_copy(way, layer, k).wait_send()

            def sent(step, carry, way=way, layer=layer):
                far_copy(way, layer, step).wait_send()
                return carry

            lax.fori_loop(1, peers, sent, 0)


def on_device(
    nodes,
    edges,
    near_table,
    far_table,
    edge_sender,
    edge_receiver,
    edge_w1,
    edge_b1,
    edge_w2,
    edge_gain,
    edge_shift,
    node_w1,
    node_b1,
    node_w2,
    node_gain,
    node_shift,
):
    peers = lax.axis_size(("node", "feat"))
    feat_size = lax.axis_size("feat")
    span, near_width = near_table.shape[1:]
    cap = far_table.shape[2]
    near_total = span * near_width
    slots = near_total + peers * cap
    padded = round_up(slots + 1, LANES)
    node_rows, features = nodes.shape
    edge_count = edges.shape[0]
    layers = edge_w1.shape[0]
    blocks = edge_count // BLOCK
    owner = jnp.concatenate(
        [near_table.reshape(1, near_total), far_table.reshape(peers, cap).T.reshape(1, peers * cap)], axis=1
    )
    owner = jnp.pad(owner, ((0, 0), (0, padded - slots)), constant_values=-1)
    senders = edge_sender.reshape(edge_count // LANES, LANES)
    receivers = edge_receiver.reshape(edge_count // LANES, LANES)
    tile = cap * features // LANES
    bf16, f32 = jnp.bfloat16, jnp.float32
    sizes = (peers, feat_size, layers, span, near_width, cap, slots)
    vmem = pl.BlockSpec(memory_space=pltpu.VMEM)
    hbm = pl.BlockSpec(memory_space=pl.ANY)
    near_buffer = pltpu.VMEM((layers, padded, features), bf16)
    far_buffer = pltpu.VMEM((layers, peers, tile, LANES), f32)
    flops = 2 * layers * edge_count * features * (2 * features + 2 * padded + slots)
    return pl.pallas_call(
        functools.partial(kernel, sizes),
        out_shape=(
            jax.ShapeDtypeStruct(nodes.shape, bf16),
            jax.ShapeDtypeStruct(edges.shape, bf16),
        ),
        in_specs=[vmem] * 10 + [hbm] * 5,
        out_specs=(vmem, hbm),
        scratch_shapes=[
            pltpu.VMEM(edge_w1.shape, bf16),
            pltpu.VMEM(edge_w2.shape, bf16),
            pltpu.VMEM(node_w1.shape, bf16),
            pltpu.VMEM(node_w2.shape, bf16),
            pltpu.VMEM(nodes.shape, bf16),
            pltpu.VMEM(edges.shape, bf16),
            pltpu.VMEM(edges.shape, f32),
            pltpu.VMEM((edge_count, 2 * padded), bf16),
            pltpu.VMEM((blocks, round_up(slots, 16), BLOCK), bf16),
            pltpu.VMEM((node_rows, padded), f32),
            pltpu.VMEM((2 * padded, features), bf16),
            pltpu.VMEM((round_up(slots, 16), features), f32),
            near_buffer, near_buffer, near_buffer, near_buffer,
            far_buffer, far_buffer, far_buffer, far_buffer,
            pltpu.SemaphoreType.DMA((1 + 4 * layers,)),
            pltpu.SemaphoreType.DMA((blocks,)),
            pltpu.SemaphoreType.DMA((2 * layers * span,)),
            pltpu.SemaphoreType.DMA((2 * layers * span,)),
            pltpu.SemaphoreType.DMA((2 * layers * peers,)),
            pltpu.SemaphoreType.DMA((2 * layers * peers,)),
        ],
        compiler_params=pltpu.CompilerParams(
            collective_id=0, has_side_effects=True, vmem_limit_bytes=50 * 2**20
        ),
        cost_estimate=pl.CostEstimate(flops=flops, bytes_accessed=12 * 2**20, transcendentals=0),
    )(
        nodes, owner, senders, receivers,
        edge_b1, edge_gain, edge_shift, node_b1, node_gain, node_shift,
        edges, edge_w1, edge_w2, node_w1, node_w2,
    )


def solution(mesh):
    split = P(AXES, None)
    table = P(AXES, None, None)
    return jax.shard_map(
        on_device,
        mesh=mesh,
        in_specs=(split, split, table, table, P(AXES), P(AXES)) + (P(),) * 10,
        out_specs=(split, split),
        check_vma=False,
    )
```

time: 171 us -> 66.2 us (0.39)
  Pallas kernels: 0 us -> 50.8 us
  starting transfers between devices: 46.9 us -> 0 us
  local copies, waits for them, and re-layouts: 56.2 us -> 13.4 us
  other arithmetic: 26.1 us -> 0.77 us
  matrix products: 24.7 us -> 0 us
  waiting for transfers between devices: 14.7 us -> 0 us
    pallas_call x0 -> x1, Pallas kernels: none -> 50.8 us  [on_device(): pl.pallas_call(functools.partial(kernel, sizes), out_shape=(jax.ShapeDtyp...]
    gather x10 -> x0, local copies, waits for them, and re-layouts: 45.3 us -> none  [the longest x3 20.7 us: on_device(): jnp.take(arrived, edge_receiver, axis=0)]
    dot_general x6 -> x0, matrix products: 24.7 us -> none  [the longest x4 21.9 us: second_half(): return jnp.dot(hidden, second_weight, preferred_element_type=jnp.float32)]
    ppermute x16 -> x0, starting transfers between devices: 24.4 us -> none  [passed_along(): return lax.ppermute(block, axis, route)]
    all_to_all x4 -> x0, starting transfers between devices: 22.5 us -> none  [the longest x2 11.7 us: on_device(): lax.all_to_all(far_sums.astype(jnp.bfloat16), ('node', 'feat'), split_axi...]
    ppermute x16 -> x0, waiting for transfers between devices: 14.7 us -> none  [passed_along(): return lax.ppermute(block, axis, route)]
    select_n x10 -> x0, other arithmetic: 9.99 us -> none  [the longest x2 4.93 us: on_device(): jnp.take(arrived, edge_sender, axis=0)]
    reduce_sum x4 -> x0, other arithmetic: 5.95 us -> none  [layer_norm(): spread = jnp.mean(center * center, axis=-1, keepdims=True)]
  transfers between devices with their start and end apart: 20 -> 0, of which waited for: 5 -> 0; matrix products, arithmetic and copies ran while one was open for 6% -> 0% of each run, Pallas kernels for 0% -> 0%
where the time goes in v1:
time: 66.2 us; the launch traced here: 65.7 us
  Pallas kernels  50.8 us (77%)
  local copies, waits for them, and re-layouts  13.4 us (20%)
  other arithmetic  0.77 us (1%)
    pallas_call x1, Pallas kernels, on_device(): pl.pallas_call(functools.partial(kernel, sizes), out_shape=(jax.ShapeDtyp...  50.8 us
    unnamed x24, local copies, waits for them, and re-layouts  12.6 us

profile of v1, /device:TPU:0, one launch (start us, length us, event | category | flops | bytes accessed | tf_op | source)
XLA Modules:
  0.0 65.7 jit_solution(8378658667478455989)
XLA Ops:
  0.6 0.8 %reshape.21 = s32[1,32]{1,0:T(1,128)S(1)} reshape(s32[2,16]{1,0:T(2,128)} %bitcast.7) | data formatting | bytes 256 | tf_op jit(solution)/shard_map/reshape | solution.py:311
  1.4 0.7 %reduce = s32[5,48]{1,0:T(8,128)S(1)} reduce(s32[1,5,48]{2,0,1:T(1,128)} %param.18, s32[]{:T(128)} %constant.6), dimensions={0}, to_apply=%param.18.reduce_sub_computation | reduce | bytes 1924 | tf_op args[2]
  2.1 0.1 reshape.19
  2.2 0.1 pad_add_fusion
  2.3 0.0 copy-start
  2.3 1.2 %copy-done = bf16[2,512,512]{2,1,0:T(8,128)(2,1)S(1)} copy-done((bf16[2,512,512]{2,1,0:T(8,128)(2,1)S(1)}, bf16[2,512,512]{2,1,0:T(8,128)(2,1)}, u32[]{:S(2)}) %copy-start) | copy-done | bytes 1048600
  3.5 0.0 copy-start.1
  3.5 1.2 %copy-done.1 = bf16[2,512,512]{2,1,0:T(8,128)(2,1)S(1)} copy-done((bf16[2,512,512]{2,1,0:T(8,128)(2,1)S(1)}, bf16[2,512,512]{2,1,0:T(8,128)(2,1)}, u32[]{:S(2)}) %copy-start.1) | copy-done | bytes 1048600
  4.7 0.0 copy-start.2
  4.7 0.9 %copy-done.2 = bf16[128,512]{1,0:T(8,128)(2,1)S(1)} copy-done((bf16[128,512]{1,0:T(8,128)(2,1)S(1)}, bf16[128,512]{1,0:T(8,128)(2,1)}, u32[]{:S(2)}) %copy-start.2) | copy-done | bytes 131096
  5.6 0.0 copy-start.3
  5.6 0.7 %copy-done.3 = s32[2048]{0:T(1024)S(1)} copy-done((s32[2048]{0:T(1024)S(1)}, s32[2048]{0:T(1024)}, u32[]{:S(2)}) %copy-start.3) | copy-done | bytes 8216
  6.3 0.0 copy-start.4
  6.3 0.7 %copy-done.4 = s32[2048]{0:T(1024)S(1)} copy-done((s32[2048]{0:T(1024)S(1)}, s32[2048]{0:T(1024)}, u32[]{:S(2)}) %copy-start.4) | copy-done | bytes 8216
  7.0 0.0 copy-start.5
  7.0 0.7 %copy-done.5 = f32[2,512]{1,0:T(2,128)S(1)} copy-done((f32[2,512]{1,0:T(2,128)S(1)}, f32[2,512]{1,0:T(2,128)}, u32[]{:S(2)}) %copy-start.5) | copy-done | bytes 4120
  7.7 0.0 copy-start.6
  7.7 0.7 %copy-done.6 = f32[2,512]{1,0:T(2,128)S(1)} copy-done((f32[2,512]{1,0:T(2,128)S(1)}, f32[2,512]{1,0:T(2,128)}, u32[]{:S(2)}) %copy-start.6) | copy-done | bytes 4120
  8.4 0.0 copy-start.7
  8.4 0.7 %copy-done.7 = f32[2,512]{1,0:T(2,128)S(1)} copy-done((f32[2,512]{1,0:T(2,128)S(1)}, f32[2,512]{1,0:T(2,128)}, u32[]{:S(2)}) %copy-start.7) | copy-done | bytes 4120
  9.1 0.0 copy-start.8
  9.1 0.7 %copy-done.8 = f32[2,512]{1,0:T(2,128)S(1)} copy-done((f32[2,512]{1,0:T(2,128)S(1)}, f32[2,512]{1,0:T(2,128)}, u32[]{:S(2)}) %copy-start.8) | copy-done | bytes 4120
  9.8 0.0 copy-start.9
  9.8 0.7 %copy-done.9 = f32[2,512]{1,0:T(2,128)S(1)} copy-done((f32[2,512]{1,0:T(2,128)S(1)}, f32[2,512]{1,0:T(2,128)}, u32[]{:S(2)}) %copy-start.9) | copy-done | bytes 4120
  10.4 0.0 copy-start.10
  10.4 0.7 %copy-done.10 = f32[2,512]{1,0:T(2,128)S(1)} copy-done((f32[2,512]{1,0:T(2,128)S(1)}, f32[2,512]{1,0:T(2,128)}, u32[]{:S(2)}) %copy-start.10) | copy-done | bytes 4120
  11.1 50.8 %shard_map.167 = (bf16[128,512]{1,0:T(8,128)(2,1)S(1)}, bf16[2048,512]{1,0:T(8,128)(2,1)}) custom-call(bf16[128,512]{1,0:T(8,128)(2,1)S(1)} %copy-done.2, s32[1,384]{1,0:T(1,128)S(1)} %pad.4.owner, s32[16,128]{1,0:T(8,128)S(1)} %bitcast.5, s32[16,128]{1,0:T(8,128)S(1)} %bitcast.6, f32[2,512]{1,0:T(2,128)S(1)} %copy-done.5, f32[2,512]{1,0:T(2,128)S(1)} %copy-done.6, ...), custom_call_target="tpu_custom_call" | custom-call | flops 8657043456 | bytes 12582912 | tf_op jit(solution)/shard_map/pallas_call | solution.py:324
  62.0 0.7 %copy.20 = bf16[128,512]{1,0:T(8,128)(2,1)} copy(bf16[128,512]{1,0:T(8,128)(2,1)S(1)} %get-tuple-element.4) | data formatting | bytes 262144
  62.6 3.0 %copy.21 = bf16[2048,512]{1,0:T(8,128)(2,1)} copy(bf16[2048,512]{1,0:T(8,128)(2,1)} %get-tuple-element.5) | data formatting | bytes 4194304
  (1 shorter events, 0.0 us)
Async XLA Ops:
  2.3 1.2 %copy-start = (bf16[2,512,512]{2,1,0:T(8,128)(2,1)S(1)}, bf16[2,512,512]{2,1,0:T(8,128)(2,1)}, u32[]{:S(2)}) copy-start(bf16[2,512,512]{2,1,0:T(8,128)(2,1)} %edge_w2_hbm.1) | copy-start | bytes 3145732
  3.5 1.2 %copy-start.1 = (bf16[2,512,512]{2,1,0:T(8,128)(2,1)S(1)}, bf16[2,512,512]{2,1,0:T(8,128)(2,1)}, u32[]{:S(2)}) copy-start(bf16[2,512,512]{2,1,0:T(8,128)(2,1)} %node_w2_hbm.1) | copy-start | bytes 3145732
  4.7 0.9 %copy-start.2 = (bf16[128,512]{1,0:T(8,128)(2,1)S(1)}, bf16[128,512]{1,0:T(8,128)(2,1)}, u32[]{:S(2)}) copy-start(bf16[128,512]{1,0:T(8,128)(2,1)} %nodes.1) | copy-start | bytes 393220
  5.6 0.7 %copy-start.3 = (s32[2048]{0:T(1024)S(1)}, s32[2048]{0:T(1024)}, u32[]{:S(2)}) copy-start(s32[2048]{0:T(1024)} %param.20) | copy-start | bytes 24580
  6.3 0.7 %copy-start.4 = (s32[2048]{0:T(1024)S(1)}, s32[2048]{0:T(1024)}, u32[]{:S(2)}) copy-start(s32[2048]{0:T(1024)} %param.21) | copy-start | bytes 24580
  7.0 0.7 %copy-start.5 = (f32[2,512]{1,0:T(2,128)S(1)}, f32[2,512]{1,0:T(2,128)}, u32[]{:S(2)}) copy-start(f32[2,512]{1,0:T(2,128)} %edge_b1.1) | copy-start | bytes 12292
  7.7 0.7 %copy-start.6 = (f32[2,512]{1,0:T(2,128)S(1)}, f32[2,512]{1,0:T(2,128)}, u32[]{:S(2)}) copy-start(f32[2,512]{1,0:T(2,128)} %edge_gain.1) | copy-start | bytes 12292
  8.4 0.7 %copy-start.7 = (f32[2,512]{1,0:T(2,128)S(1)}, f32[2,512]{1,0:T(2,128)}, u32[]{:S(2)}) copy-start(f32[2,512]{1,0:T(2,128)} %edge_shift.1) | copy-start | bytes 12292
  9.1 0.7 %copy-start.8 = (f32[2,512]{1,0:T(2,128)S(1)}, f32[2,512]{1,0:T(2,128)}, u32[]{:S(2)}) copy-start(f32[2,512]{1,0:T(2,128)} %node_b1.1) | copy-start | bytes 12292
  9.8 0.7 %copy-start.9 = (f32[2,512]{1,0:T(2,128)S(1)}, f32[2,512]{1,0:T(2,128)}, u32[]{:S(2)}) copy-start(f32[2,512]{1,0:T(2,128)} %node_gain.1) | copy-start | bytes 12292
  10.4 0.7 %copy-start.10 = (f32[2,512]{1,0:T(2,128)S(1)}, f32[2,512]{1,0:T(2,128)}, u32[]{:S(2)}) copy-start(f32[2,512]{1,0:T(2,128)} %node_shift.1) | copy-start | bytes 12292

commit v2 on v1

--- a/solution.py
+++ b/solution.py
@@ -22,8 +22,7 @@
     return jnp.dot(a, b, preferred_element_type=jnp.float32)
 
 
-def layer_norm(values, norm_gain, norm_shift):
-    center = values - jnp.mean(values, axis=-1, keepdims=True)
+def layer_norm(center, norm_gain, norm_shift):
     spread = jnp.mean(center * center, axis=-1, keepdims=True)
     return center * lax.rsqrt(spread + EPSILON) * norm_gain + norm_shift
 
@@ -34,12 +33,15 @@
 
 def kernel(
     sizes,
-    nodes, owner, senders, receivers,
+    nodes_hbm, near_hbm, far_hbm, senders_hbm, receivers_hbm,
+    edge_b1_hbm, edge_gain_hbm, edge_shift_hbm, node_b1_hbm, node_gain_hbm, node_shift_hbm,
+    edges_hbm, edge_w1_hbm, edge_w2_hbm, node_w1_hbm, node_w2_hbm,
+    states, edge_out,
+    edges,
+    near_table, far_table, senders, receivers,
     edge_b1, edge_gain, edge_shift, node_b1, node_gain, node_shift,
-    edges_hbm, edge_w1_hbm, edge_w2_hbm, node_w1_hbm, node_w2_hbm,
-    node_out, edge_out,
     edge_w1, edge_w2, node_w1, node_w2,
-    states, edges, partial, hot, hot_t, owner_t, projected, sums,
+    partial, hidden_even, hidden_odd, hot, hot_t, pick, projected, sums,
     near_out, near_in, near_back_out, near_back_in,
     far_out, far_in, far_back_out, far_back_in,
     load_sems, store_sems,
@@ -48,7 +50,7 @@
     peers, feat_size, layers, span, near_width, cap, slots = sizes
     reach = (span - 1) // 2
     near_total = span * near_width
-    padded = owner_t.shape[1]
+    padded = pick.shape[0]
     features = states.shape[1]
     columns = features // LANES
     edge_count = edges.shape[0]
@@ -59,16 +61,28 @@
     def device(index):
         return (ens, index // feat_size, index % feat_size)
 
-    loads = [pltpu.make_async_copy(edges_hbm, edges, load_sems.at[0])]
-    for layer in range(layers):
-        for place, (source, target) in enumerate(
-            ((edge_w1_hbm, edge_w1), (edge_w2_hbm, edge_w2), (node_w1_hbm, node_w1), (node_w2_hbm, node_w2))
-        ):
-            loads.append(
-                pltpu.make_async_copy(source.at[layer], target.at[layer], load_sems.at[1 + 4 * layer + place])
-            )
-    for load in loads:
-        load.start()
+    loads = []
+
+    def load(source, target):
+        copy = pltpu.make_async_copy(source, target, load_sems.at[len(loads)])
+        copy.start()
+        loads.append(copy)
+        return copy
+
+    first_loads = [load(nodes_hbm, states), load(near_hbm, near_table), load(far_hbm, far_table)]
+    index_loads = [load(senders_hbm, senders), load(receivers_hbm, receivers)]
+    own_loads = [load(edge_b1_hbm, edge_b1), load(edges_hbm, edges), load(edge_w1_hbm.at[0], edge_w1.at[0])]
+    late_loads = [
+        load(edge_gain_hbm, edge_gain),
+        load(edge_shift_hbm, edge_shift),
+        load(node_b1_hbm, node_b1),
+        load(node_gain_hbm, node_gain),
+        load(node_shift_hbm, node_shift),
+        load(edge_w2_hbm, edge_w2),
+        load(node_w1_hbm, node_w1),
+        load(node_w2_hbm, node_w2),
+    ]
+    late_loads += [load(edge_w1_hbm.at[layer], edge_w1.at[layer]) for layer in range(1, layers)]
 
     barrier = pltpu.get_barrier_semaphore()
 
@@ -78,13 +92,21 @@
 
     lax.fori_loop(1, peers, greet, 0)
 
+    for copy in first_loads:
+        copy.wait()
     node_rows = states.shape[0]
-    row_ids = lax.broadcasted_iota(jnp.int32, (node_rows, LANES), 0)
-    for j in range(padded // LANES):
-        picked = owner[:, j * LANES : (j + 1) * LANES] == row_ids
-        owner_t[:, j * LANES : (j + 1) * LANES] = jnp.where(picked, 1.0, 0.0)
-
-    states[...] = nodes[...]
+    near_ids = lax.broadcasted_iota(jnp.int32, (near_width, node_rows), 1).astype(jnp.float32)
+    far_ids = lax.broadcasted_iota(jnp.int32, (peers, node_rows), 1).astype(jnp.float32)
+    for k in range(span):
+        row = near_table[k].astype(jnp.float32)
+        column = jnp.transpose(jnp.broadcast_to(row, (node_rows, near_width)))
+        pick[k * near_width : (k + 1) * near_width, :] = jnp.where(column == near_ids, 1.0, 0.0)
+    for s in range(cap):
+        begin = near_total + s * peers
+        row = far_table[s : s + 1, :].astype(jnp.float32)
+        column = jnp.transpose(jnp.broadcast_to(row, (node_rows, peers)))
+        pick[begin : begin + peers, :] = jnp.where(column == far_ids, 1.0, 0.0)
+    pick[slots:, :] = jnp.zeros((padded - slots, node_rows), jnp.float32)
 
     def near_copy(way, layer, k):
         source, target = ((near_out, near_in), (near_back_out, near_back_in))[way]
@@ -169,8 +191,11 @@
                 ].astype(jnp.bfloat16)
 
     def gathered():
-        pick = jnp.transpose(owner_t[...]).astype(jnp.bfloat16)
-        return dot(pick, states[...])
+        return dot(pick[...].astype(jnp.bfloat16), states[...])
+
+    def store(i):
+        rows = pl.ds(pl.multiple_of(i * BLOCK, BLOCK), BLOCK)
+        return pltpu.make_async_copy(edges.at[rows], edge_out.at[rows], store_sems.at[i])
 
     send(0, 0, gathered(), first=True)
 
@@ -180,6 +205,8 @@
         peer = jnp.floor((far + 0.5) * (1.0 / cap))
         return jnp.where(value < near_total, value, near_total + (far - peer * cap) * peers + peer)
 
+    for copy in index_loads:
+        copy.wait()
     sender_ids = renumbered(senders[...])
     receiver_ids = renumbered(receivers[...])
     lane_ids = lax.broadcasted_iota(jnp.int32, (LANES, LANES), 1).astype(jnp.float32)
@@ -198,11 +225,9 @@
             receiver_ids[b : b + 1] == slot_ids, 1.0, 0.0
         ).astype(jnp.bfloat16)
 
-    loads[0].wait()
+    for copy in own_loads:
+        copy.wait()
     for layer in range(layers):
-        for place in range(4):
-            if layer == 0 and place == 0:
-                loads[1].wait()
 
         def own_term(i, carry, layer=layer):
             rows = pl.ds(pl.multiple_of(i * BLOCK, BLOCK), BLOCK)
@@ -213,8 +238,12 @@
 
         if layer == 0:
             lax.fori_loop(0, blocks, own_term, 0)
-            for load in loads[2:]:
-                load.wait()
+            for copy in late_loads:
+                copy.wait()
+            for weight in (edge_w2, node_w2):
+                for place in range(layers):
+                    values = weight[place].astype(jnp.float32)
+                    weight[place] = (values - jnp.mean(values, axis=-1, keepdims=True)).astype(jnp.bfloat16)
 
         receive(0, layer)
         arrived = near_in[layer]
@@ -226,28 +255,45 @@
 
         sums[...] = jnp.zeros_like(sums)
 
-        def update(i, carry, layer=layer):
-            rows = pl.ds(pl.multiple_of(i * BLOCK, BLOCK), BLOCK)
-            half = partial[rows, :] + dot(hot[rows, :], projected[...])
-            mixed = dot(gated(half), edge_w2[layer])
+        def block_rows(i):
+            return pl.ds(pl.multiple_of(i * BLOCK, BLOCK), BLOCK)
+
+        def first_half(i, hidden):
+            rows = block_rows(i)
+            hidden[...] = gated(partial[rows, :] + dot(hot[rows, :], projected[...]))
+
+        def second_half(i, hidden, layer=layer):
+            rows = block_rows(i)
+            mixed = dot(hidden[...], edge_w2[layer])
             fresh = edges[rows, :].astype(jnp.float32) + layer_norm(
                 mixed, edge_gain[layer : layer + 1, :], edge_shift[layer : layer + 1, :]
             )
             fresh = fresh.astype(jnp.bfloat16)
             edges[rows, :] = fresh
             if layer == layers - 1:
-                pltpu.make_async_copy(edges.at[rows], edge_out.at[rows], store_sems.at[i]).start()
+                store(i).start()
             sums[...] += dot(hot_t[i], fresh)
+
+        first_half(0, hidden_even)
+
+        def update(j, carry):
+            first_half(2 * j + 1, hidden_odd)
+            second_half(2 * j, hidden_even)
+            first_half(2 * j + 2, hidden_even)
+            second_half(2 * j + 1, hidden_odd)
             return carry
 
-        lax.fori_loop(0, blocks, update, 0)
+        lax.fori_loop(0, blocks // 2 - 1, update, 0)
+        first_half(blocks - 1, hidden_odd)
+        second_half(blocks - 2, hidden_even)
+        second_half(blocks - 1, hidden_odd)
 
         send(1, layer, sums)
         pre = dot(states[...], node_w1[layer, :features, :]) + node_b1[layer : layer + 1, :]
         if layer + 1 < layers:
             lax.fori_loop(0, blocks, functools.partial(own_term, layer=layer + 1), 0)
         receive(1, layer)
-        aggregate = dot(owner_t[...].astype(jnp.bfloat16), near_back_in[layer]).astype(jnp.bfloat16)
+        aggregate = dot(jnp.transpose(pick[...]).astype(jnp.bfloat16), near_back_in[layer]).astype(jnp.bfloat16)
         half = 0.5 * (pre + dot(aggregate, node_w1[layer, features:, :]))
         mixed = dot(gated(half), node_w2[layer])
         fresh = states[...].astype(jnp.float32) + layer_norm(
@@ -257,11 +303,8 @@
         if layer + 1 < layers:
             send(0, layer + 1, gathered())
 
-    node_out[...] = states[...]
-
     def drain(i, carry):
-        rows = pl.ds(pl.multiple_of(i * BLOCK, BLOCK), BLOCK)
-        pltpu.make_async_copy(edges.at[rows], edge_out.at[rows], store_sems.at[i]).wait()
+        store(i).wait()
         return carry
 
     lax.fori_loop(0, blocks, drain, 0)
@@ -301,23 +344,21 @@
     span, near_width = near_table.shape[1:]
     cap = far_table.shape[2]
     near_total = span * near_width
+    near_table = jnp.transpose(near_table, (1, 0, 2))
+    far_table = far_table.reshape(peers, cap).T
     slots = near_total + peers * cap
     padded = round_up(slots + 1, LANES)
     node_rows, features = nodes.shape
     edge_count = edges.shape[0]
     layers = edge_w1.shape[0]
     blocks = edge_count // BLOCK
-    owner = jnp.concatenate(
-        [near_table.reshape(1, near_total), far_table.reshape(peers, cap).T.reshape(1, peers * cap)], axis=1
-    )
-    owner = jnp.pad(owner, ((0, 0), (0, padded - slots)), constant_values=-1)
     senders = edge_sender.reshape(edge_count // LANES, LANES)
     receivers = edge_receiver.reshape(edge_count // LANES, LANES)
     tile = cap * features // LANES
     bf16, f32 = jnp.bfloat16, jnp.float32
     sizes = (peers, feat_size, layers, span, near_width, cap, slots)
     vmem = pl.BlockSpec(memory_space=pltpu.VMEM)
-    hbm = pl.BlockSpec(memory_space=pl.ANY)
+    hbm = pl.BlockSpec(memory_space=pltpu.HBM)
     near_buffer = pltpu.VMEM((layers, padded, features), bf16)
     far_buffer = pltpu.VMEM((layers, peers, tile, LANES), f32)
     flops = 2 * layers * edge_count * features * (2 * features + 2 * padded + slots)
@@ -327,24 +368,32 @@
             jax.ShapeDtypeStruct(nodes.shape, bf16),
             jax.ShapeDtypeStruct(edges.shape, bf16),
         ),
-        in_specs=[vmem] * 10 + [hbm] * 5,
+        in_specs=[hbm] * 16,
         out_specs=(vmem, hbm),
         scratch_shapes=[
+            pltpu.VMEM(edges.shape, bf16),
+            pltpu.VMEM(near_table.shape, jnp.int32),
+            pltpu.VMEM(far_table.shape, jnp.int32),
+            pltpu.VMEM(senders.shape, jnp.int32),
+            pltpu.VMEM(receivers.shape, jnp.int32),
+        ]
+        + [pltpu.VMEM(edge_b1.shape, f32)] * 6
+        + [
             pltpu.VMEM(edge_w1.shape, bf16),
             pltpu.VMEM(edge_w2.shape, bf16),
             pltpu.VMEM(node_w1.shape, bf16),
             pltpu.VMEM(node_w2.shape, bf16),
-            pltpu.VMEM(nodes.shape, bf16),
-            pltpu.VMEM(edges.shape, bf16),
             pltpu.VMEM(edges.shape, f32),
+            pltpu.VMEM((BLOCK, features), bf16),
+            pltpu.VMEM((BLOCK, features), bf16),
             pltpu.VMEM((edge_count, 2 * padded), bf16),
             pltpu.VMEM((blocks, round_up(slots, 16), BLOCK), bf16),
-            pltpu.VMEM((node_rows, padded), f32),
+            pltpu.VMEM((padded, node_rows), f32),
             pltpu.VMEM((2 * padded, features), bf16),
             pltpu.VMEM((round_up(slots, 16), features), f32),
             near_buffer, near_buffer, near_buffer, near_buffer,
             far_buffer, far_buffer, far_buffer, far_buffer,
-            pltpu.SemaphoreType.DMA((1 + 4 * layers,)),
+            pltpu.SemaphoreType.DMA((15 + layers,)),
             pltpu.SemaphoreType.DMA((blocks,)),
             pltpu.SemaphoreType.DMA((2 * layers * span,)),
             pltpu.SemaphoreType.DMA((2 * layers * span,)),
@@ -352,11 +401,11 @@
             pltpu.SemaphoreType.DMA((2 * layers * peers,)),
         ],
         compiler_params=pltpu.CompilerParams(
-            collective_id=0, has_side_effects=True, vmem_limit_bytes=50 * 2**20
+            collective_id=0, has_side_effects=True, vmem_limit_bytes=62 * 2**20
         ),
         cost_estimate=pl.CostEstimate(flops=flops, bytes_accessed=12 * 2**20, transcendentals=0),
     )(
-        nodes, owner, senders, receivers,
+        nodes, near_table, far_table, senders, receivers,
         edge_b1, edge_gain, edge_shift, node_b1, node_gain, node_shift,
         edges, edge_w1, edge_w2, node_w1, node_w2,
     )

time: 66.2 us -> 52.8 us (0.80)
  local copies, waits for them, and re-layouts: 13.4 us -> 4.61 us
  Pallas kernels: 50.8 us -> 47.4 us
  other arithmetic: 0.77 us -> 0 us
    unnamed x24 -> x2, local copies, waits for them, and re-layouts: 12.6 us -> 4.61 us
    pallas_call x1, Pallas kernels: 50.8 us -> 47.4 us  [on_device(): pl.pallas_call(functools.partial(kernel, sizes), out_shape=(jax.ShapeDtyp...]
    reshape x2 -> x0, local copies, waits for them, and re-layouts: 0.84 us -> none  [the longest x1 0.76 us: on_device(): far_table.reshape(peers, cap).T.reshape(1, peers * cap)]
    unnamed x1 -> x0, other arithmetic: 0.7 us -> none
where the time goes in v2:
time: 52.8 us; the launch traced here: 52.7 us
  Pallas kernels  47.4 us (90%)
  local copies, waits for them, and re-layouts  4.61 us (9%)
  between operations  0.65 us (1%)
    pallas_call x1, Pallas kernels, on_device(): pl.pallas_call(functools.partial(kernel, sizes), out_shape=(jax.ShapeDtyp...  47.4 us
    unnamed x2, local copies, waits for them, and re-layouts  4.61 us

profile of v2, /device:TPU:0, one launch (start us, length us, event | category | flops | bytes accessed | tf_op | source)
XLA Modules:
  0.0 52.7 jit_solution(2205259061078394351)
XLA Ops:
  0.6 47.4 %shard_map.167 = (bf16[128,512]{1,0:T(8,128)(2,1)}, bf16[2048,512]{1,0:T(8,128)(2,1)}) custom-call(bf16[128,512]{1,0:T(8,128)(2,1)} %nodes_hbm.1, s32[5,1,48]{2,1,0:T(1,128)} %bitcast.8, s32[2,16]{1,0:T(2,128)} %bitcast.9, s32[16,128]{1,0:T(8,128)} %bitcast.6, s32[16,128]{1,0:T(8,128)} %bitcast.7, f32[2,512]{1,0:T(2,128)} %edge_b1_hbm.1, ...), custom_call_target="tpu_custom_call" | custom-call | flops 8657043456 | bytes 12582912 | tf_op jit(solution)/shard_map/pallas_call | solution.py:365
  48.1 1.6 %copy.20 = bf16[128,512]{1,0:T(8,128)(2,1)} copy(bf16[128,512]{1,0:T(8,128)(2,1)} %get-tuple-element.4) | data formatting | bytes 262144
  49.6 3.0 %copy.21 = bf16[2048,512]{1,0:T(8,128)(2,1)} copy(bf16[2048,512]{1,0:T(8,128)(2,1)} %get-tuple-element.5) | data formatting | bytes 4194304

commit v3 on v2

--- a/solution.py
+++ b/solution.py
@@ -44,6 +44,7 @@
     partial, hidden_even, hidden_odd, hot, hot_t, pick, projected, sums,
     near_out, near_in, near_back_out, near_back_in,
     far_out, far_in, far_back_out, far_back_in,
+    far_rows,
     load_sems, store_sems,
     near_send, near_recv, far_send, far_recv,
 ):
@@ -59,7 +60,10 @@
     me = lax.axis_index("node") * feat_size + lax.axis_index("feat")
 
     def device(index):
-        return (ens, index // feat_size, index % feat_size)
+        return (ens, lax.div(index, feat_size), lax.rem(index, feat_size))
+
+    def around(index):
+        return jnp.where(index >= peers, index - peers, index)
 
     loads = []
 
@@ -87,7 +91,7 @@
     barrier = pltpu.get_barrier_semaphore()
 
     def greet(step, carry):
-        pl.semaphore_signal(barrier, inc=1, device_id=device((me + step) % peers), device_id_type=MESH)
+        pl.semaphore_signal(barrier, inc=1, device_id=device(around(me + step)), device_id_type=MESH)
         return carry
 
     lax.fori_loop(1, peers, greet, 0)
@@ -118,13 +122,13 @@
             dst_ref=target.at[layer, rows],
             send_sem=near_send.at[slot],
             recv_sem=near_recv.at[slot],
-            device_id=device((me + shift + peers) % peers),
+            device_id=device(around(me + (shift + peers) % peers)),
             device_id_type=MESH,
         )
 
     def far_copy(way, layer, step):
         source, target = ((far_out, far_in), (far_back_out, far_back_in))[way]
-        to = (me + step) % peers
+        to = around(me + step)
         slot = (way * layers + layer) * peers + step
         return pltpu.make_async_remote_copy(
             src_ref=source.at[layer, to],
@@ -137,7 +141,7 @@
 
     def far_arrival(way, layer, step):
         source, target = ((far_out, far_in), (far_back_out, far_back_in))[way]
-        origin = (me + peers - step) % peers
+        origin = around(me + peers - step)
         slot = (way * layers + layer) * peers + step
         return pltpu.make_async_remote_copy(
             src_ref=source.at[layer, origin],
@@ -155,7 +159,8 @@
         for s in range(cap):
             begin = near_total + s * peers
             for c in range(columns):
-                far_source[layer, :, s * columns + c, :] = rows[begin : begin + peers, c * LANES : (c + 1) * LANES]
+                far_rows[:, s * columns + c, :] = rows[begin : begin + peers, c * LANES : (c + 1) * LANES]
+        far_source[layer] = far_rows[...].astype(jnp.bfloat16)
         if first:
             pl.semaphore_wait(barrier, peers - 1)
         for k in range(span):
@@ -183,11 +188,12 @@
             return carry
 
         lax.fori_loop(1, peers, wait, 0)
+        far_rows[...] = far_target[layer].astype(jnp.float32)
         for s in range(cap):
             begin = near_total + s * peers
             for c in range(columns):
-                target[layer, begin : begin + peers, c * LANES : (c + 1) * LANES] = far_target[
-                    layer, :, s * columns + c, :
+                target[layer, begin : begin + peers, c * LANES : (c + 1) * LANES] = far_rows[
+                    :, s * columns + c, :
                 ].astype(jnp.bfloat16)
 
     def gathered():
@@ -319,6 +325,22 @@
                 return carry
 
             lax.fori_loop(1, peers, sent, 0)
+
+
+def handed_on(nodes_in, edges_in, nodes_out, edges_out, nodes_held, edges_held, sems):
+    pieces = [(nodes_in, nodes_held, nodes_out)]
+    for begin in range(0, edges_in.shape[0], BLOCK):
+        rows = pl.ds(begin, BLOCK)
+        pieces.append((edges_in.at[rows], edges_held.at[rows], edges_out.at[rows]))
+    fetches = [pltpu.make_async_copy(a, b, sems.at[0, i]) for i, (a, b, _) in enumerate(pieces)]
+    writes = [pltpu.make_async_copy(b, c, sems.at[1, i]) for i, (_, b, c) in enumerate(pieces)]
+    for fetch in fetches:
+        fetch.start()
+    for fetch, write in zip(fetches, writes):
+        fetch.wait()
+        write.start()
+    for write in writes:
+        write.wait()
 
 
 def on_device(
@@ -360,14 +382,15 @@
     vmem = pl.BlockSpec(memory_space=pltpu.VMEM)
     hbm = pl.BlockSpec(memory_space=pltpu.HBM)
     near_buffer = pltpu.VMEM((layers, padded, features), bf16)
-    far_buffer = pltpu.VMEM((layers, peers, tile, LANES), f32)
+    far_buffer = pltpu.VMEM((layers, peers, tile, LANES), bf16)
     flops = 2 * layers * edge_count * features * (2 * features + 2 * padded + slots)
-    return pl.pallas_call(
+    out_shape = (
+        jax.ShapeDtypeStruct(nodes.shape, bf16),
+        jax.ShapeDtypeStruct(edges.shape, bf16),
+    )
+    results = pl.pallas_call(
         functools.partial(kernel, sizes),
-        out_shape=(
-            jax.ShapeDtypeStruct(nodes.shape, bf16),
-            jax.ShapeDtypeStruct(edges.shape, bf16),
-        ),
+        out_shape=out_shape,
         in_specs=[hbm] * 16,
         out_specs=(vmem, hbm),
         scratch_shapes=[
@@ -393,6 +416,7 @@
             pltpu.VMEM((round_up(slots, 16), features), f32),
             near_buffer, near_buffer, near_buffer, near_buffer,
             far_buffer, far_buffer, far_buffer, far_buffer,
+            pltpu.VMEM((peers, tile, LANES), f32),
             pltpu.SemaphoreType.DMA((15 + layers,)),
             pltpu.SemaphoreType.DMA((blocks,)),
             pltpu.SemaphoreType.DMA((2 * layers * span,)),
@@ -409,6 +433,19 @@
         edge_b1, edge_gain, edge_shift, node_b1, node_gain, node_shift,
         edges, edge_w1, edge_w2, node_w1, node_w2,
     )
+    return pl.pallas_call(
+        handed_on,
+        out_shape=out_shape,
+        in_specs=[hbm] * 2,
+        out_specs=(hbm, hbm),
+        scratch_shapes=[
+            pltpu.VMEM(nodes.shape, bf16),
+            pltpu.VMEM(edges.shape, bf16),
+            pltpu.SemaphoreType.DMA((2, 1 + blocks)),
+        ],
+        compiler_params=pltpu.CompilerParams(vmem_limit_bytes=62 * 2**20),
+        cost_estimate=pl.CostEstimate(flops=0, bytes_accessed=2 * 2 * (nodes.size + edges.size), transcendentals=0),
+    )(*results)
 
 
 def solution(mesh):

time: 52.8 us -> 49.4 us (0.936)
  local copies, waits for them, and re-layouts: 4.61 us -> 0 us
  Pallas kernels: 47.4 us -> 48.6 us
    unnamed x2 -> x0, local copies, waits for them, and re-layouts: 4.61 us -> none
    pallas_call x1 -> x2, Pallas kernels: 47.4 us -> 48.6 us  [the longest x1 46.1 us: on_device(): pl.pallas_call(functools.partial(kernel, sizes), out_shape=out_shape, in_...]
where the time goes in v3:
time: 49.4 us; the launch traced here: 49.3 us
  Pallas kernels  48.6 us (98%)
  between operations  0.64 us (1%)
    pallas_call x1, Pallas kernels, on_device(): pl.pallas_call(functools.partial(kernel, sizes), out_shape=out_shape, in_...  46.1 us
    pallas_call x1, Pallas kernels, on_device(): pl.pallas_call(handed_on, out_shape=out_shape, in_specs=[hbm] * 2, out_sp...  2.48 us

profile of v3, /device:TPU:0, one launch (start us, length us, event | category | flops | bytes accessed | tf_op | source)
XLA Modules:
  0.0 49.3 jit_solution(16883756727468656028)
XLA Ops:
  0.6 46.1 %shard_map.167 = (bf16[128,512]{1,0:T(8,128)(2,1)}, bf16[2048,512]{1,0:T(8,128)(2,1)}) custom-call(bf16[128,512]{1,0:T(8,128)(2,1)} %nodes_hbm.1, s32[5,1,48]{2,1,0:T(1,128)} %bitcast.8, s32[2,16]{1,0:T(2,128)} %bitcast.9, s32[16,128]{1,0:T(8,128)} %bitcast.6, s32[16,128]{1,0:T(8,128)} %bitcast.7, f32[2,512]{1,0:T(2,128)} %edge_b1_hbm.1, ...), custom_call_target="tpu_custom_call" | custom-call | flops 8657043456 | bytes 12582912 | tf_op jit(solution)/shard_map/pallas_call | solution.py:391
  46.8 2.5 %shard_map.168 = (bf16[128,512]{1,0:T(8,128)(2,1)}, bf16[2048,512]{1,0:T(8,128)(2,1)}) custom-call(bf16[128,512]{1,0:T(8,128)(2,1)} %get-tuple-element.4.nodes_in, bf16[2048,512]{1,0:T(8,128)(2,1)} %get-tuple-element.5.edges_in), custom_call_target="tpu_custom_call" | custom-call | bytes 4456448 | tf_op jit(solution)/shard_map/pallas_call | solution.py:436

commit v4 on v3

--- a/solution.py
+++ b/solution.py
@@ -9,7 +9,7 @@
 
 EPSILON = 1e-05
 LANES = 128
-BLOCK = 256
+BLOCK = 512
 AXES = ("ens", "node", "feat")
 MESH = pl.DeviceIdType.MESH
 
@@ -200,7 +200,7 @@
         return dot(pick[...].astype(jnp.bfloat16), states[...])
 
     def store(i):
-        rows = pl.ds(pl.multiple_of(i * BLOCK, BLOCK), BLOCK)
+        rows = pl.ds(i * BLOCK, BLOCK)
         return pltpu.make_async_copy(edges.at[rows], edge_out.at[rows], store_sems.at[i])
 
     send(0, 0, gathered(), first=True)
@@ -262,7 +262,7 @@
         sums[...] = jnp.zeros_like(sums)
 
         def block_rows(i):
-            return pl.ds(pl.multiple_of(i * BLOCK, BLOCK), BLOCK)
+            return pl.ds(i * BLOCK, BLOCK)
 
         def first_half(i, hidden):
             rows = block_rows(i)
@@ -280,19 +280,12 @@
                 store(i).start()
             sums[...] += dot(hot_t[i], fresh)
 
-        first_half(0, hidden_even)
-
-        def update(j, carry):
-            first_half(2 * j + 1, hidden_odd)
-            second_half(2 * j, hidden_even)
-            first_half(2 * j + 2, hidden_even)
-            second_half(2 * j + 1, hidden_odd)
-            return carry
-
-        lax.fori_loop(0, blocks // 2 - 1, update, 0)
-        first_half(blocks - 1, hidden_odd)
-        second_half(blocks - 2, hidden_even)
-        second_half(blocks - 1, hidden_odd)
+        held = (hidden_even, hidden_odd)
+        first_half(0, held[0])
+        for i in range(blocks):
+            if i + 1 < blocks:
+                first_half(i + 1, held[(i + 1) % 2])
+            second_half(i, held[i % 2])
 
         send(1, layer, sums)
         pre = dot(states[...], node_w1[layer, :features, :]) + node_b1[layer : layer + 1, :]
@@ -309,11 +302,8 @@
         if layer + 1 < layers:
             send(0, layer + 1, gathered())
 
-    def drain(i, carry):
+    for i in range(blocks):
         store(i).wait()
-        return carry
-
-    lax.fori_loop(0, blocks, drain, 0)
     for way in range(2):
         for layer in range(layers):
             for k in range(span):

time: 49.4 us -> 46.2 us (0.935)
  Pallas kernels: 48.6 us -> 45.4 us
    pallas_call x1, Pallas kernels: 46.1 us -> 42.8 us  [on_device(): pl.pallas_call(functools.partial(kernel, sizes), out_shape=out_shape, in_...]
where the time goes in v4:
time: 46.2 us; the launch traced here: 46 us
  Pallas kernels  45.4 us (98%)
  between operations  0.64 us (1%)
    pallas_call x1, Pallas kernels, on_device(): pl.pallas_call(functools.partial(kernel, sizes), out_shape=out_shape, in_...  42.8 us
    pallas_call x1, Pallas kernels, on_device(): pl.pallas_call(handed_on, out_shape=out_shape, in_specs=[hbm] * 2, out_sp...  2.51 us

profile of v4, /device:TPU:0, one launch (start us, length us, event | category | flops | bytes accessed | tf_op | source)
XLA Modules:
  0.0 46.0 jit_solution(7043311969264182877)
XLA Ops:
  0.6 42.8 %shard_map.167 = (bf16[128,512]{1,0:T(8,128)(2,1)}, bf16[2048,512]{1,0:T(8,128)(2,1)}) custom-call(bf16[128,512]{1,0:T(8,128)(2,1)} %nodes_hbm.1, s32[5,1,48]{2,1,0:T(1,128)} %bitcast.8, s32[2,16]{1,0:T(2,128)} %bitcast.9, s32[16,128]{1,0:T(8,128)} %bitcast.6, s32[16,128]{1,0:T(8,128)} %bitcast.7, f32[2,512]{1,0:T(2,128)} %edge_b1_hbm.1, ...), custom_call_target="tpu_custom_call" | custom-call | flops 8657043456 | bytes 12582912 | tf_op jit(solution)/shard_map/pallas_call | solution.py:381
  43.5 2.5 %shard_map.168 = (bf16[128,512]{1,0:T(8,128)(2,1)}, bf16[2048,512]{1,0:T(8,128)(2,1)}) custom-call(bf16[128,512]{1,0:T(8,128)(2,1)} %get-tuple-element.4.nodes_in, bf16[2048,512]{1,0:T(8,128)(2,1)} %get-tuple-element.5.edges_in), custom_call_target="tpu_custom_call" | custom-call | bytes 4456448 | tf_op jit(solution)/shard_map/pallas_call | solution.py:426

commit v5 on v4

--- a/solution.py
+++ b/solution.py
@@ -10,6 +10,7 @@
 EPSILON = 1e-05
 LANES = 128
 BLOCK = 512
+OWN_BLOCK = 1024
 AXES = ("ens", "node", "feat")
 MESH = pl.DeviceIdType.MESH
 
@@ -56,6 +57,7 @@
     columns = features // LANES
     edge_count = edges.shape[0]
     blocks = edge_count // BLOCK
+    own_blocks = edge_count // OWN_BLOCK
     ens = lax.axis_index("ens")
     me = lax.axis_index("node") * feat_size + lax.axis_index("feat")
 
@@ -156,16 +158,16 @@
         source, far_source = ((near_out, far_out), (near_back_out, far_back_out))[way]
         target, far_target = ((near_in, far_in), (near_back_in, far_back_in))[way]
         source[layer, :near_total, :] = rows[:near_total].astype(jnp.bfloat16)
+        if first:
+            pl.semaphore_wait(barrier, peers - 1)
+        for k in range(span):
+            if k != reach:
+                near_copy(way, layer, k).start()
         for s in range(cap):
             begin = near_total + s * peers
             for c in range(columns):
                 far_rows[:, s * columns + c, :] = rows[begin : begin + peers, c * LANES : (c + 1) * LANES]
         far_source[layer] = far_rows[...].astype(jnp.bfloat16)
-        if first:
-            pl.semaphore_wait(barrier, peers - 1)
-        for k in range(span):
-            if k != reach:
-                near_copy(way, layer, k).start()
 
         def start(step, carry):
             far_copy(way, layer, step).start()
@@ -213,43 +215,48 @@
 
     for copy in index_loads:
         copy.wait()
-    sender_ids = renumbered(senders[...])
+    tiles = edge_count // LANES
     receiver_ids = renumbered(receivers[...])
+    spread_rows = lax.broadcasted_iota(jnp.int32, (2 * tiles, LANES), 0)
     lane_ids = lax.broadcasted_iota(jnp.int32, (LANES, LANES), 1).astype(jnp.float32)
     slot_ids = lax.broadcasted_iota(jnp.int32, (hot_t.shape[1], LANES), 0).astype(jnp.float32)
-    for b in range(edge_count // LANES):
-        rows = slice(b * LANES, (b + 1) * LANES)
-        for side, ids in enumerate((sender_ids, receiver_ids)):
-            column = jnp.transpose(jnp.broadcast_to(ids[b : b + 1], (LANES, LANES)))
+    for side, ids in enumerate((renumbered(senders[...]), receiver_ids)):
+        high = 256.0 * jnp.floor(ids * (1.0 / 256.0))
+        parts = jnp.transpose(jnp.concatenate([high, ids - high], axis=0)).astype(jnp.bfloat16)
+        for b in range(tiles):
+            chosen = (spread_rows == b) | (spread_rows == tiles + b)
+            column = dot(parts, jnp.where(chosen, 1.0, 0.0).astype(jnp.bfloat16))
             for j in range(padded // LANES):
                 begin = side * padded + j * LANES
-                hot[rows, begin : begin + LANES] = jnp.where(column == lane_ids + j * LANES, 1.0, 0.0).astype(
-                    jnp.bfloat16
-                )
+                hot[b * LANES : (b + 1) * LANES, begin : begin + LANES] = jnp.where(
+                    column == lane_ids + j * LANES, 1.0, 0.0
+                ).astype(jnp.bfloat16)
+    for b in range(tiles):
         begin = (b * LANES) % BLOCK
         hot_t[b * LANES // BLOCK, :, begin : begin + LANES] = jnp.where(
             receiver_ids[b : b + 1] == slot_ids, 1.0, 0.0
         ).astype(jnp.bfloat16)
 
+    def centre(weight, layer):
+        values = weight[layer].astype(jnp.float32)
+        weight[layer] = (values - jnp.mean(values, axis=-1, keepdims=True)).astype(jnp.bfloat16)
+
     for copy in own_loads:
         copy.wait()
     for layer in range(layers):
 
         def own_term(i, carry, layer=layer):
-            rows = pl.ds(pl.multiple_of(i * BLOCK, BLOCK), BLOCK)
+            rows = pl.ds(pl.multiple_of(i * OWN_BLOCK, OWN_BLOCK), OWN_BLOCK)
             partial[rows, :] = 0.5 * (
                 dot(edges[rows, :], edge_w1[layer, :features, :]) + edge_b1[layer : layer + 1, :]
             )
             return carry
 
         if layer == 0:
-            lax.fori_loop(0, blocks, own_term, 0)
+            lax.fori_loop(0, own_blocks, own_term, 0)
             for copy in late_loads:
                 copy.wait()
-            for weight in (edge_w2, node_w2):
-                for place in range(layers):
-                    values = weight[place].astype(jnp.float32)
-                    weight[place] = (values - jnp.mean(values, axis=-1, keepdims=True)).astype(jnp.bfloat16)
+            centre(edge_w2, 0)
 
         receive(0, layer)
         arrived = near_in[layer]
@@ -288,9 +295,11 @@
             second_half(i, held[i % 2])
 
         send(1, layer, sums)
+        centre(node_w2, layer)
         pre = dot(states[...], node_w1[layer, :features, :]) + node_b1[layer : layer + 1, :]
         if layer + 1 < layers:
-            lax.fori_loop(0, blocks, functools.partial(own_term, layer=layer + 1), 0)
+            centre(edge_w2, layer + 1)
+            lax.fori_loop(0, own_blocks, functools.partial(own_term, layer=layer + 1), 0)
         receive(1, layer)
         aggregate = dot(jnp.transpose(pick[...]).astype(jnp.bfloat16), near_back_in[layer]).astype(jnp.bfloat16)
         half = 0.5 * (pre + dot(aggregate, node_w1[layer, features:, :]))

time: 46.2 us -> 46.1 us (level)
  no operation moved by 1% of the time
where the time goes in v5:
time: 46.1 us; the launch traced here: 45.9 us
  Pallas kernels  45.3 us (98%)
  between operations  0.64 us (1%)
    pallas_call x1, Pallas kernels, on_device(): pl.pallas_call(functools.partial(kernel, sizes), out_shape=out_shape, in_...  42.8 us
    pallas_call x1, Pallas kernels, on_device(): pl.pallas_call(handed_on, out_shape=out_shape, in_specs=[hbm] * 2, out_sp...  2.51 us

profile of v5, /device:TPU:0, one launch (start us, length us, event | category | flops | bytes accessed | tf_op | source)
XLA Modules:
  0.0 45.9 jit_solution(3916913124233598148)
XLA Ops:
  0.6 42.8 %shard_map.167 = (bf16[128,512]{1,0:T(8,128)(2,1)}, bf16[2048,512]{1,0:T(8,128)(2,1)}) custom-call(bf16[128,512]{1,0:T(8,128)(2,1)} %nodes_hbm.1, s32[5,1,48]{2,1,0:T(1,128)} %bitcast.8, s32[2,16]{1,0:T(2,128)} %bitcast.9, s32[16,128]{1,0:T(8,128)} %bitcast.6, s32[16,128]{1,0:T(8,128)} %bitcast.7, f32[2,512]{1,0:T(2,128)} %edge_b1_hbm.1, ...), custom_call_target="tpu_custom_call" | custom-call | flops 8657043456 | bytes 12582912 | tf_op jit(solution)/shard_map/pallas_call | solution.py:390
  43.4 2.5 %shard_map.168 = (bf16[128,512]{1,0:T(8,128)(2,1)}, bf16[2048,512]{1,0:T(8,128)(2,1)}) custom-call(bf16[128,512]{1,0:T(8,128)(2,1)} %get-tuple-element.4.nodes_in, bf16[2048,512]{1,0:T(8,128)(2,1)} %get-tuple-element.5.edges_in), custom_call_target="tpu_custom_call" | custom-call | bytes 4456448 | tf_op jit(solution)/shard_map/pallas_call | solution.py:435

commit v6 on v5

--- a/solution.py
+++ b/solution.py
@@ -37,8 +37,8 @@
     nodes_hbm, near_hbm, far_hbm, senders_hbm, receivers_hbm,
     edge_b1_hbm, edge_gain_hbm, edge_shift_hbm, node_b1_hbm, node_gain_hbm, node_shift_hbm,
     edges_hbm, edge_w1_hbm, edge_w2_hbm, node_w1_hbm, node_w2_hbm,
-    states, edge_out,
-    edges,
+    aggregate_out, states_out, pre_out, weight_out, edge_out,
+    states, pre, edges,
     near_table, far_table, senders, receivers,
     edge_b1, edge_gain, edge_shift, node_b1, node_gain, node_shift,
     edge_w1, edge_w2, node_w1, node_w2,
@@ -46,7 +46,7 @@
     near_out, near_in, near_back_out, near_back_in,
     far_out, far_in, far_back_out, far_back_in,
     far_rows,
-    load_sems, store_sems,
+    load_sems, store_sems, node_sems,
     near_send, near_recv, far_send, far_recv,
 ):
     peers, feat_size, layers, span, near_width, cap, slots = sizes
@@ -181,6 +181,15 @@
 
     def receive(way, layer):
         target, far_target = ((near_in, far_in), (near_back_in, far_back_in))[way]
+
+        def sent(step, carry):
+            far_copy(way, layer, step).wait_send()
+            return carry
+
+        lax.fori_loop(1, peers, sent, 0)
+        for k in range(span):
+            if k != reach:
+                near_copy(way, layer, k).wait_send()
         for k in range(span):
             if k != reach:
                 near_copy(way, layer, k).wait_recv()
@@ -296,48 +305,81 @@
 
         send(1, layer, sums)
         centre(node_w2, layer)
-        pre = dot(states[...], node_w1[layer, :features, :]) + node_b1[layer : layer + 1, :]
+        pre[...] = dot(states[...], node_w1[layer, :features, :]) + node_b1[layer : layer + 1, :]
+        if layer == layers - 1:
+            node_stores = [
+                pltpu.make_async_copy(states, states_out, node_sems.at[0]),
+                pltpu.make_async_copy(pre, pre_out, node_sems.at[1]),
+                pltpu.make_async_copy(node_w2.at[layer], weight_out, node_sems.at[2]),
+            ]
+            for copy in node_stores:
+                copy.start()
         if layer + 1 < layers:
             centre(edge_w2, layer + 1)
             lax.fori_loop(0, own_blocks, functools.partial(own_term, layer=layer + 1), 0)
         receive(1, layer)
         aggregate = dot(jnp.transpose(pick[...]).astype(jnp.bfloat16), near_back_in[layer]).astype(jnp.bfloat16)
-        half = 0.5 * (pre + dot(aggregate, node_w1[layer, features:, :]))
+        if layer == layers - 1:
+            aggregate_out[...] = aggregate
+            break
+        half = 0.5 * (pre[...] + dot(aggregate, node_w1[layer, features:, :]))
         mixed = dot(gated(half), node_w2[layer])
         fresh = states[...].astype(jnp.float32) + layer_norm(
             mixed, node_gain[layer : layer + 1, :], node_shift[layer : layer + 1, :]
         )
         states[...] = fresh.astype(jnp.bfloat16)
-        if layer + 1 < layers:
-            send(0, layer + 1, gathered())
-
+        send(0, layer + 1, gathered())
+
+    for copy in node_stores:
+        copy.wait()
     for i in range(blocks):
         store(i).wait()
-    for way in range(2):
-        for layer in range(layers):
-            for k in range(span):
-                if k != reach:
-                    near_copy(way, layer, k).wait_send()
-
-            def sent(step, carry, way=way, layer=layer):
-                far_copy(way, layer, step).wait_send()
-                return carry
-
-            lax.fori_loop(1, peers, sent, 0)
-
-
-def handed_on(nodes_in, edges_in, nodes_out, edges_out, nodes_held, edges_held, sems):
-    pieces = [(nodes_in, nodes_held, nodes_out)]
-    for begin in range(0, edges_in.shape[0], BLOCK):
-        rows = pl.ds(begin, BLOCK)
-        pieces.append((edges_in.at[rows], edges_held.at[rows], edges_out.at[rows]))
-    fetches = [pltpu.make_async_copy(a, b, sems.at[0, i]) for i, (a, b, _) in enumerate(pieces)]
-    writes = [pltpu.make_async_copy(b, c, sems.at[1, i]) for i, (_, b, c) in enumerate(pieces)]
-    for fetch in fetches:
-        fetch.start()
-    for fetch, write in zip(fetches, writes):
+
+
+def last_step(
+    aggregate_hbm, states_hbm, pre_hbm, weight_hbm, node_w1_hbm, gain_hbm, shift_hbm, edges_hbm,
+    node_out, edge_out,
+    aggregate, states, pre, second, first, gain, shift, edges,
+    sems, fetch_sems, write_sems,
+):
+    layer = gain.shape[0] - 1
+    features = states.shape[1]
+    loads = [
+        pltpu.make_async_copy(source, target, sems.at[i])
+        for i, (source, target) in enumerate(
+            (
+                (aggregate_hbm, aggregate),
+                (node_w1_hbm.at[layer, pl.ds(features, features)], first),
+                (pre_hbm, pre),
+                (weight_hbm, second),
+                (states_hbm, states),
+                (gain_hbm, gain),
+                (shift_hbm, shift),
+            )
+        )
+    ]
+    fetches, writes = [], []
+    for i in range(edges.shape[0] // LANES):
+        rows = pl.ds(i * LANES, LANES)
+        fetches.append(pltpu.make_async_copy(edges_hbm.at[rows], edges.at[rows], fetch_sems.at[i]))
+        writes.append(pltpu.make_async_copy(edges.at[rows], edge_out.at[rows], write_sems.at[i]))
+    for copy in loads + fetches:
+        copy.start()
+    for copy in loads:
+        copy.wait()
+    middle = len(fetches) // 2
+    for fetch, write in zip(fetches[:middle], writes[:middle]):
         fetch.wait()
         write.start()
+    half = 0.5 * (pre[...] + dot(aggregate[...], first[...]))
+    mixed = dot(gated(half), second[...])
+    for fetch, write in zip(fetches[middle:], writes[middle:]):
+        fetch.wait()
+        write.start()
+    fresh = states[...].astype(jnp.float32) + layer_norm(
+        mixed, gain[layer : layer + 1, :], shift[layer : layer + 1, :]
+    )
+    node_out[...] = fresh.astype(jnp.bfloat16)
     for write in writes:
         write.wait()
 
@@ -387,12 +429,20 @@
         jax.ShapeDtypeStruct(nodes.shape, bf16),
         jax.ShapeDtypeStruct(edges.shape, bf16),
     )
-    results = pl.pallas_call(
+    aggregate, states, pre, weight, edge_state = pl.pallas_call(
         functools.partial(kernel, sizes),
-        out_shape=out_shape,
+        out_shape=(
+            out_shape[0],
+            out_shape[0],
+            jax.ShapeDtypeStruct(nodes.shape, f32),
+            jax.ShapeDtypeStruct(node_w2.shape[1:], bf16),
+            out_shape[1],
+        ),
         in_specs=[hbm] * 16,
-        out_specs=(vmem, hbm),
+        out_specs=(vmem, hbm, hbm, hbm, hbm),
         scratch_shapes=[
+            pltpu.VMEM(nodes.shape, bf16),
+            pltpu.VMEM(nodes.shape, f32),
             pltpu.VMEM(edges.shape, bf16),
             pltpu.VMEM(near_table.shape, jnp.int32),
             pltpu.VMEM(far_table.shape, jnp.int32),
@@ -418,6 +468,7 @@
             pltpu.VMEM((peers, tile, LANES), f32),
             pltpu.SemaphoreType.DMA((15 + layers,)),
             pltpu.SemaphoreType.DMA((blocks,)),
+            pltpu.SemaphoreType.DMA((3,)),
             pltpu.SemaphoreType.DMA((2 * layers * span,)),
             pltpu.SemaphoreType.DMA((2 * layers * span,)),
             pltpu.SemaphoreType.DMA((2 * layers * peers,)),
@@ -433,18 +484,26 @@
         edges, edge_w1, edge_w2, node_w1, node_w2,
     )
     return pl.pallas_call(
-        handed_on,
+        last_step,
         out_shape=out_shape,
-        in_specs=[hbm] * 2,
-        out_specs=(hbm, hbm),
+        in_specs=[hbm] * 8,
+        out_specs=(vmem, hbm),
         scratch_shapes=[
             pltpu.VMEM(nodes.shape, bf16),
+            pltpu.VMEM(nodes.shape, bf16),
+            pltpu.VMEM(nodes.shape, f32),
+            pltpu.VMEM(node_w2.shape[1:], bf16),
+            pltpu.VMEM(node_w2.shape[1:], bf16),
+            pltpu.VMEM(node_gain.shape, f32),
+            pltpu.VMEM(node_shift.shape, f32),
             pltpu.VMEM(edges.shape, bf16),
-            pltpu.SemaphoreType.DMA((2, 1 + blocks)),
+            pltpu.SemaphoreType.DMA((7,)),
+            pltpu.SemaphoreType.DMA((edge_count // LANES,)),
+            pltpu.SemaphoreType.DMA((edge_count // LANES,)),
         ],
         compiler_params=pltpu.CompilerParams(vmem_limit_bytes=62 * 2**20),
         cost_estimate=pl.CostEstimate(flops=0, bytes_accessed=2 * 2 * (nodes.size + edges.size), transcendentals=0),
-    )(*results)
+    )(aggregate, states, pre, weight, node_w1, node_gain, node_shift, edge_state)
 
 
 def solution(mesh):

time: 46.1 us -> 47 us (1.020)
  Pallas kernels: 45.3 us -> 46.2 us
    pallas_call x2, Pallas kernels: 45.3 us -> 46.2 us  [the longest x1 41.9 us: on_device(): pl.pallas_call(functools.partial(kernel, sizes), out_shape=(out_shape[0],...]
where the time goes in v6:
time: 47 us; the launch traced here: 46.9 us
  Pallas kernels  46.2 us (98%)
  between operations  0.64 us (1%)
    pallas_call x1, Pallas kernels, on_device(): pl.pallas_call(functools.partial(kernel, sizes), out_shape=(out_shape[0],...  41.9 us
    pallas_call x1, Pallas kernels, on_device(): pl.pallas_call(last_step, out_shape=out_shape, in_specs=[hbm] * 8, out_sp...  4.36 us

profile of v6, /device:TPU:0, one launch (start us, length us, event | category | flops | bytes accessed | tf_op | source)
XLA Modules:
  0.0 46.9 jit_solution(13786114110877889573)
XLA Ops:
  0.6 41.9 %shard_map.167 = (bf16[128,512]{1,0:T(8,128)(2,1)}, bf16[128,512]{1,0:T(8,128)(2,1)}, f32[128,512]{1,0:T(8,128)}, bf16[512,512]{1,0:T(8,128)(2,1)}, bf16[2048,512]{1,0:T(8,128)(2,1)}) custom-call(bf16[128,512]{1,0:T(8,128)(2,1)} %nodes_hbm.1, s32[5,1,48]{2,1,0:T(1,128)} %bitcast.8, s32[2,16]{1,0:T(2,128)} %bitcast.9, s32[16,128]{1,0:T(8,128)} %bitcast.6, ...), custom_call_target="tpu_custom_call" | custom-call | flops 8657043456 | bytes 12582912 | tf_op jit(solution)/shard_map/pallas_call | solution.py:432
  42.5 4.4 %shard_map.168 = (bf16[128,512]{1,0:T(8,128)(2,1)}, bf16[2048,512]{1,0:T(8,128)(2,1)}) custom-call(bf16[128,512]{1,0:T(8,128)(2,1)} %get-tuple-element.7.aggregate_hbm, bf16[128,512]{1,0:T(8,128)(2,1)} %get-tuple-element.8.states_hbm, f32[128,512]{1,0:T(8,128)} %get-tuple-element.9.pre_hbm, bf16[512,512]{1,0:T(8,128)(2,1)} %get-tuple-element.10.weight_hbm, ...), custom_call_target="tpu_custom_call" | custom-call | bytes 4456448 | tf_op jit(solution)/shard_map/pallas_call | solution.py:486
